TPU v7x, 32 devices: a whole 2x2x4 slice. The times are simulated.
32 devices in a mesh: row: 4 (over y, x), col: 8 (over z, core).
Axes of the slice: x: 2, y: 2, z: 4, core: 2. Of those that a mesh axis runs over, the one named last changes fastest.
Arguments:
- upper_blocks: bfloat16 [4, 8, 63, 128, 128], P('row', 'col'), may hold values from -1.5 to 1.5
- block_targets: int32 [4, 8, 63], P('row', 'col'), may hold values from 0 to 7, as said below
- product_plan: int32 [4, 8, 2, 128, 3], P('row', 'col'), may hold values from 0 to 125, as said below
- live_counts: int32 [4, 8, 2], P('row', 'col'), may hold values from 24 to 128, as said below
Outputs:
- result_blocks: bfloat16 [4, 8, 32, 128, 128], P('row', 'col')
Inputs may be any that keep to these rules, and one draw needn't show every extreme that they name: `block_targets`: A device's stored blocks never target its own column; within one grid row, the k-th stored block of every device targets the same number of columns onward, and at most 9 of a device's blocks target one column, reached in every draw. `product_plan`: columns 0 and 1 name panel blocks below 126, column 2 a result block below 32. In section 1, all 128 slots of a device together name exactly 24 distinct left blocks and exactly 24 distinct right blocks. `live_counts`: in each section some device has all 128 slots live.
All inputs are finite; a program needn't handle non-finite values.
Results may differ from a plain program's by a relative error of at most 0.008.
Values may be sent and summed in bfloat16 or wider, within the bound.
No kernel may reach another device: no remote copies, remote signals or barrier semaphores. Data moves between devices by JAX's collectives and lax.ppermute only.
A program may use at most 64 MiB of HBM per device.

v0:
```python
import functools

import jax
import jax.numpy as jnp
from jax import lax
from jax.experimental import pallas as pl
from jax.experimental.pallas import tpu as pltpu
from jax.sharding import PartitionSpec as P

OUTSLOTS = 32
USED = 24
UNROLL = 16
NEXT_UNROLL = 32
FIRST = 1
LEFT_PIECES = 1
RIGHT_PIECES = 1
FIRST_MIB = 61
MIB = 1 << 20

SMEM = pl.BlockSpec(memory_space=pltpu.SMEM)
VMEM = pl.BlockSpec(memory_space=pltpu.VMEM)
HBM = pl.BlockSpec(memory_space=pltpu.HBM)


def cost(us):
    return pl.CostEstimate(flops=0, bytes_accessed=int(us * 3.5e6), transcendentals=0)


def i32(*shape):
    return jax.ShapeDtypeStruct(shape, jnp.int32)


def params(mib):
    return pltpu.CompilerParams(vmem_limit_bytes=mib * MIB)


def moved(value, axis, steps):
    count = lax.axis_size(axis)
    return lax.ppermute(value, axis, [(s, (s + steps) % count) for s in range(count)])


def after(value, *needed):
    return lax.optimization_barrier((value, *needed))[0]


class Order:
    def __init__(self, token):
        self.token = token

    def gate(self, value):
        value, self.token = lax.optimization_barrier((value, self.token))
        return value


class Layout:
    def __init__(self, stored, cols):
        self.stored = stored
        self.cols = cols
        self.cap = (stored + cols - 2) // (cols - 1)
        half = cols // 2
        others = [d for d in range(2, cols) if d != half]
        others.sort(key=lambda d: (half - abs(d - half), d))
        others = others[1:2] + others[:1] + others[2:3] + others[3:]
        pieces = min(5, len(others))
        cuts = [len(others) * i // pieces for i in range(pieces + 1)]
        groups = [others[a:b] for a, b in zip(cuts, cuts[1:])]
        self.stages = groups[:3] + [[1]] + groups[3:] + [[half]]
        self.base = [0] * cols
        self.start = []
        at = 0
        for stage in self.stages:
            self.start.append(at)
            for d in stage:
                self.base[d] = at
                at += self.cap
        self.total = at
        self.start.append(at)
        self.self_stage = self.stages.index([1])

    def size(self, s):
        return self.start[s + 1] - self.start[s]


def offset_of(lay, tgt, k, me):
    d = tgt[k] - me
    return jnp.where(d < 0, d + lay.cols, d)


def first_kernel(lay, tgt, col, stored_ref, *rest):
    outs, (buf, found, sem) = rest[:FIRST], rest[FIRST:]
    goals = []
    for n, offset in enumerate(d for stage in lay.stages[:FIRST] for d in stage):
        goal = col[0] + offset
        goals.append(jnp.where(goal >= lay.cols, goal - lay.cols, goal))
    at = [jnp.int32(n * lay.cap) for n in range(len(goals))]
    for k in range(lay.stored):
        target = tgt[k]
        for n, goal in enumerate(goals):
            hit = target == goal
            found[jnp.where(hit, at[n], lay.total)] = k
            at[n] = at[n] + hit.astype(jnp.int32)
    total = lay.start[FIRST]
    for j in range(total):
        pltpu.make_async_copy(stored_ref.at[found[j]], buf.at[j], sem).start()
    pltpu.make_async_copy(buf, buf, sem).wait()
    for s, out in enumerate(outs):
        for j in range(lay.size(s)):
            out[j] = buf[lay.start[s] + j].T


def first_stage(lay, targets, col, stored):
    block = stored.shape[-1]
    return pl.pallas_call(
        functools.partial(first_kernel, lay),
        out_shape=tuple(jax.ShapeDtypeStruct((lay.size(s), block, block), stored.dtype) for s in range(FIRST)),
        in_specs=[SMEM, SMEM, HBM],
        out_specs=(VMEM,) * FIRST,
        scratch_shapes=[
            pltpu.VMEM((lay.start[FIRST], block, block), stored.dtype),
            pltpu.SMEM((lay.total + 1,), jnp.int32),
            pltpu.SemaphoreType.DMA,
        ],
        compiler_params=params(FIRST_MIB),
        name="first_stage",
    )(targets, col, stored)


def rest_kernel(lay, tgt, col, plan, stored_ref, *rest):
    outs, pos, inv, cnt = rest[:-3], rest[-3], rest[-2], rest[-1]
    for d in range(lay.cols):
        cnt[d] = lay.base[d]

    def place(k, carry):
        d = offset_of(lay, tgt, k, col[0])
        q = cnt[d]
        cnt[d] = q + 1
        pos[k] = q
        inv[q] = k
        return carry

    lax.fori_loop(0, lay.stored, place, 0)
    for s in range(FIRST, len(lay.stages)):

        def flip(j, carry, s=s):
            outs[s - FIRST][j] = stored_ref[inv[lay.start[s] + j]].T
            return carry

        lax.fori_loop(0, lay.size(s), flip, 0, unroll=9 if lay.size(s) % 9 == 0 else 1)
    note = outs[lay.self_stage - FIRST]
    block = note.shape[-1]
    for row in range(plan.shape[2] // block):
        line = plan[0, 1:2, row * block : row * block + block].astype(jnp.float32)
        note[lay.size(lay.self_stage), row * 16 : row * 16 + 16, :] = jnp.broadcast_to(line, (16, block)).astype(note.dtype)


def rest_stages(lay, targets, col, plan, stored):
    block = stored.shape[-1]
    shapes = tuple(
        jax.ShapeDtypeStruct((lay.size(s) + (s == lay.self_stage), block, block), stored.dtype)
        for s in range(FIRST, len(lay.stages))
    )
    return pl.pallas_call(
        functools.partial(rest_kernel, lay),
        out_shape=shapes + (i32(lay.stored),),
        in_specs=[SMEM, SMEM, VMEM, VMEM],
        out_specs=(VMEM,) * len(shapes) + (SMEM,),
        scratch_shapes=[pltpu.SMEM((lay.total,), jnp.int32), pltpu.SMEM((lay.cols,), jnp.int32)],
        compiler_params=params(12),
        cost_estimate=cost(0.01),
        name="rest_stages",
    )(targets, col, plan, stored)


def wanted_kernel(prods, plan, reqs_r, slots_l, slots_r, seen_l, seen_r):
    def clear(i, carry):
        seen_l[i] = -1
        seen_r[i] = -1
        return carry

    lax.fori_loop(0, seen_l.shape[0], clear, 0, unroll=6 if seen_l.shape[0] % 6 == 0 else 1)
    for i in range(USED):
        reqs_r[i] = 0

    def step(p, counts):
        sides = ((slots_l, seen_l), (slots_r, seen_r))
        found = [plan[side, 1, p] for side in range(2)]
        known = [seen[which] for (_, seen), which in zip(sides, found)]
        slot = [jnp.where(k < 0, n, k) for k, n in zip(known, counts)]
        for (slots, seen), which, at in zip(sides, found, slot):
            seen[which] = at
            slots[p] = at
        reqs_r[slot[1]] = found[1]
        return tuple(n + (k < 0).astype(jnp.int32) for k, n in zip(known, counts))

    lax.fori_loop(0, prods, step, (jnp.int32(0), jnp.int32(0)), unroll=4)


def wanted(panel_size, plan, prods):
    return pl.pallas_call(
        functools.partial(wanted_kernel, prods),
        out_shape=(i32(USED), i32(prods), i32(prods)),
        in_specs=[SMEM],
        out_specs=(SMEM,) * 3,
        scratch_shapes=[pltpu.SMEM((panel_size,), jnp.int32)] * 2,
        cost_estimate=cost(0.01),
        name="wanted",
    )(plan)


def panel_place(lay, pos, which):
    lower = which >= lay.stored
    return jnp.where(lower, lay.stored + pos[jnp.where(lower, which - lay.stored, 0)], which)


def asked_kernel(lay, ids, pos, spots, seen):
    def clear(i, carry):
        seen[i] = 0
        return carry

    lax.fori_loop(0, seen.shape[0], clear, 0, unroll=6 if seen.shape[0] % 6 == 0 else 1)

    def step(p, n):
        which = ids[p]
        known = seen[which]
        spots[n] = panel_place(lay, pos, which)
        seen[which] = 1
        return n + 1 - known

    lax.fori_loop(0, ids.shape[0], step, jnp.int32(0), unroll=4)


def asked(lay, ids, pos):
    return pl.pallas_call(
        functools.partial(asked_kernel, lay),
        out_shape=i32(USED + 1),
        in_specs=[SMEM, SMEM],
        out_specs=SMEM,
        scratch_shapes=[pltpu.SMEM((2 * lay.stored,), jnp.int32)],
        name="asked",
    )(ids, pos)


def pick_kernel(lay, stages, pieces, spots, stored_ref, *rest):
    parts, outs = rest[: len(stages)], rest[len(stages) :]
    size = USED // pieces
    for piece, out in enumerate(outs):
        for n in range(size):
            q = spots[piece * size + n] - lay.stored
            value = stored_ref[jnp.minimum(q + lay.stored, lay.stored - 1)]
            for s, part in zip(stages, parts):
                at = jnp.clip(q - lay.start[s], 0, lay.size(s) - 1)
                value = jnp.where(q >= lay.start[s], part[at], value)
            out[n] = value


def pick(lay, stages, pieces, spots, stored, parts, name):
    block = stored.shape[-1]
    return pl.pallas_call(
        functools.partial(pick_kernel, lay, stages, pieces),
        out_shape=(jax.ShapeDtypeStruct((USED // pieces, block, block), stored.dtype),) * pieces,
        in_specs=[SMEM, VMEM] + [VMEM] * len(parts),
        out_specs=(VMEM,) * pieces,
        compiler_params=params(16),
        name=name,
    )(spots, stored, *parts)


def multiply(count, entry, left, right, acc):
    spare = acc.shape[0] - 1

    def group(g, carry):
        found = []
        for u in range(UNROLL):
            p = g * UNROLL + u
            i, j, o = entry(p)
            o = jnp.where(p < count, o, spare)
            found.append((o, jnp.dot(left[i], right[j], preferred_element_type=jnp.float32)))
        for o, term in found:
            acc[o] += term
        return carry

    lax.fori_loop(0, (count + UNROLL - 1) // UNROLL, group, 0)


def own_kernel(lay, prods, plan, counts, pos, stored_ref, *rest):
    parts = rest[: len(lay.stages)]
    acc, panel, sem = rest[len(lay.stages) :]
    copies = [pltpu.make_async_copy(stored_ref, panel.at[pl.ds(0, lay.stored)], sem.at[0])]
    for s, part in enumerate(parts):
        copies.append(
            pltpu.make_async_copy(
                part.at[pl.ds(0, lay.size(s))], panel.at[pl.ds(lay.stored + lay.start[s], lay.size(s))], sem.at[s + 1]
            )
        )
    for copy in copies:
        copy.start()

    def zero(o, carry):
        acc[o] = jnp.zeros(acc.shape[1:], acc.dtype)
        return carry

    lax.fori_loop(0, acc.shape[0], zero, 0)
    for copy in copies:
        copy.wait()

    def where(which):
        lower = which >= lay.stored
        return jnp.where(lower, lay.stored + pos[jnp.where(lower, which - lay.stored, 0)], which)

    def entry(p):
        return where(plan[0, 0, p]), where(plan[1, 0, p]), plan[2, 0, p]

    multiply(counts[0], entry, panel, panel, acc)


def own_section(lay, plan, counts, pos, stored, parts):
    block = stored.shape[-1]
    prods = plan.shape[2]
    return pl.pallas_call(
        functools.partial(own_kernel, lay, prods),
        out_shape=jax.ShapeDtypeStruct((OUTSLOTS + 1, block, block), jnp.float32),
        in_specs=[SMEM, SMEM, SMEM, VMEM] + [VMEM] * len(parts),
        out_specs=VMEM,
        scratch_shapes=[
            pltpu.VMEM((lay.stored + lay.total, block, block), stored.dtype),
            pltpu.SemaphoreType.DMA((len(parts) + 1,)),
        ],
        compiler_params=params(20),
        cost_estimate=cost(0.01),
        name="own_section",
    )(plan, counts, pos, stored, *parts)


def places_kernel(lay, late, plan, counts, slots_l, slots_r, pos, pos_r, asked_r, out, spots):
    for n in range(USED):
        spots[n] = panel_place(lay, pos, asked_r[n])
    own_from, own_to = lay.start[lay.self_stage], lay.start[lay.self_stage + 1]
    late_from = lay.start[late[0]]

    def step(p, carry):
        left_id, right_id = plan[0, 1, p], plan[1, 1, p]
        lower = left_id >= lay.stored
        q = pos[jnp.where(lower, left_id - lay.stored, 0)]
        out[0, p] = jnp.where(lower & (q >= own_from) & (q < own_to), USED + q - own_from, slots_l[p])
        lower = right_id >= lay.stored
        q = pos_r[jnp.where(lower, right_id - lay.stored, 0)]
        out[1, p] = jnp.where(lower & (q >= late_from), USED + q - late_from, slots_r[p])
        out[2, p] = jnp.where(p < counts[1], plan[2, 1, p], OUTSLOTS)
        return carry

    lax.fori_loop(0, plan.shape[2], step, 0, unroll=4)


def places(lay, late, plan, counts, slots_l, slots_r, pos, pos_r, asked_r):
    return pl.pallas_call(
        functools.partial(places_kernel, lay, late),
        out_shape=(i32(3, plan.shape[2]), i32(USED)),
        in_specs=[SMEM] * 7,
        out_specs=(SMEM, SMEM),
        name="places",
    )(plan, counts, slots_l, slots_r, pos, pos_r, asked_r)


def either(n, first, first_size, others):
    value = first[jnp.minimum(n, first_size - 1)]
    at = first_size
    for part, size in others:
        value = jnp.where(n >= at, part[jnp.clip(n - at, 0, size - 1)], value)
        at += size
    return value


def next_kernel(lay, late, token, spots, counts, old, self_ref, left, right, *rest):
    parts, (acc, out) = rest[:-2], rest[-2:]
    lefts = [(self_ref, lay.size(lay.self_stage))]
    rights = [(part, lay.size(s)) for s, part in zip(late, parts)]

    def group(g, carry):
        found = []
        for u in range(NEXT_UNROLL):
            p = g * NEXT_UNROLL + u
            i, j, o = spots[0, p], spots[1, p], spots[2, p]
            a = either(i, left, USED, lefts)
            b = either(j, right, USED, rights)
            found.append((o, jnp.dot(a, b, preferred_element_type=jnp.float32)))
        for o, term in found:
            acc[o] += term
        return carry

    lax.fori_loop(0, (counts[1] + NEXT_UNROLL - 1) // NEXT_UNROLL, group, 0)
    for o in range(OUTSLOTS):
        out[o] = acc[o].astype(out.dtype)


def next_section(lay, late, token, spots, counts, acc, self_part, left, right, parts):
    block = self_part.shape[-1]
    return pl.pallas_call(
        functools.partial(next_kernel, lay, late),
        out_shape=(
            jax.ShapeDtypeStruct(acc.shape, acc.dtype),
            jax.ShapeDtypeStruct((OUTSLOTS, block, block), self_part.dtype),
        ),
        in_specs=[SMEM] * 3 + [VMEM] * (4 + len(parts)),
        out_specs=(VMEM, VMEM),
        input_output_aliases={3: 0},
        compiler_params=params(20),
        cost_estimate=cost(0.01),
        name="next_section",
    )(token, spots, counts, acc, self_part, left, right, *parts)[1]


FLIGHT = 2
EARLY = 6


def body(upper_blocks, block_targets, product_plan, live_counts):
    stored = upper_blocks[0, 0]
    targets = block_targets[0, 0]
    counts = live_counts[0, 0]
    plan = jnp.transpose(product_plan[0, 0], (2, 0, 1))
    prods = plan.shape[2]
    lay = Layout(stored.shape[0], lax.axis_size("col"))
    stages = list(range(len(lay.stages)))
    early, late = stages[:EARLY], stages[EARLY:]
    col = lax.axis_index("col").astype(jnp.int32).reshape(1)

    def exchange(s, send):
        if len(lay.stages[s]) == 1:
            return moved(send, "col", lay.stages[s][0])
        parts = [
            moved(send[n * lay.cap : (n + 1) * lay.cap], "col", d) for n, d in enumerate(lay.stages[s])
        ]
        return jnp.concatenate(parts, axis=0)

    order = Order(col)
    sends = list(order.gate(first_stage(lay, targets, col, stored)))
    got = [exchange(s, sends[s]) for s in range(FIRST)]
    *rest, pos = rest_stages(lay, targets, col, plan, order.gate(stored))
    sends += rest
    got += [exchange(s, sends[s]) for s in stages[FIRST:-1]]
    for s in stages[:2]:
        got[s] = order.gate(got[s])
    reqs_r, slots_l, slots_r = order.gate(wanted(2 * lay.stored, order.gate(plan), prods))
    asked_r = moved(reqs_r, "row", 1)
    pos_r = moved(pos, "row", -1)
    asked_r, pos_r = order.gate((asked_r, pos_r))
    spots, asked_r = order.gate(places(lay, late, order.gate(plan), counts, slots_l, slots_r, pos, pos_r, asked_r))
    got[2] = order.gate(got[2])
    got[3] = order.gate(got[3])
    rows = prods // stored.shape[-1]
    ids = got[lay.self_stage][-1, : 16 * rows : 16].reshape(-1).astype(jnp.int32)
    asked_l = order.gate(asked(lay, order.gate(ids), pos))
    for s in stages[4:-1]:
        got[s] = order.gate(got[s])
    got.append(exchange(stages[-1], order.gate(sends[-1])))
    picked = order.gate(pick(lay, early, RIGHT_PIECES, asked_r, stored, [got[s] for s in early], "pick_right"))
    right = [moved(piece, "row", -1) for piece in picked]
    got[-1] = order.gate(got[-1])
    forwarded = [moved(got[s], "row", -1) for s in late]
    ready = [s for s in stages if s != lay.self_stage]
    picked = pick(lay, ready, LEFT_PIECES, order.gate(asked_l), stored, [got[s] for s in ready], "pick_left")
    left = [moved(piece, "col", -1) for piece in order.gate(picked)]
    acc = own_section(lay, plan, counts, pos, stored, got)
    out = next_section(lay, late, order.token, spots, counts, acc, sends[lay.self_stage], *left, *right, forwarded)
    return out[None, None]


def solution(mesh):
    placed = (
        P("row", "col", None, None, None),
        P("row", "col", None),
        P("row", "col", None, None, None),
        P("row", "col", None),
    )
    return jax.shard_map(
        body,
        mesh=mesh,
        in_specs=placed,
        out_specs=P("row", "col", None, None, None),
        check_vma=False,
    )
```

profile of v0, /device:TPU:31, one launch (start us, length us, event | category | flops | bytes accessed | tf_op | source)
XLA Modules:
  0.0 79.4 jit_solution(2931771779628767410)
XLA Ops:
  0.0 2.7 %first_stage.1 = bf16[9,128,128]{2,1,0:T(8,128)(2,1)} custom-call(s32[63]{0:T(128)} %bitcast.23, s32[1]{0:T(128)} %bitcast.1.col.token, bf16[63,128,128]{2,1,0:T(8,128)(2,1)} %bitcast.11), custom_call_target="tpu_custom_call" | custom-call | tf_op jit(solution)/shard_map/first_stage/pallas_call | solution.py:113
  2.7 0.1 collective-permute-start.3
  2.8 2.9 %rest_stages.1 = (bf16[9,128,128]{2,1,0:T(8,128)(2,1)S(1)}, bf16[9,128,128]{2,1,0:T(8,128)(2,1)}, bf16[10,128,128]{2,1,0:T(8,128)(2,1)}, bf16[9,128,128]{2,1,0:T...) custom-call(s32[63]{0:T(128)S(1)} %bitcast.24, s32[1]{0:T(128)} %bitcast.1.col.token, ...), custom_call_target="tpu_custom_call" | custom-call | bytes 35000 | tf_op jit(solution)/shard_map/rest_stages/pallas_call | solution.py:162
  5.8 0.7 copy-done.10
  6.5 2.0 %collective-permute-start = (bf16[10,128,128]{2,1,0:T(8,128)(2,1)}, bf16[10,128,128]{2,1,0:T(8,128)(2,1)}, u32[]{:S(2)}, u32[]{:S(2)}) collective-permute-start(bf16[10,128,128]{2,1,0:T(8,128)(2,1)} %get-tuple-element.64.self_ref), channel_id=1, source_target_pairs={{0,1},{1,2},{2,3},{3,4},{4,5},{5,6},{6,7},{7,0},{8,9},{9,10},{10,1... | collective-permute-start | bytes 983048 | tf_op jit(solution)/shard_map/ppermute | solution.py:39
  8.6 0.3 collective-permute-start.1
  8.9 3.8 %collective-permute-start.7 = (bf16[9,128,128]{2,1,0:T(8,128)(2,1)}, bf16[9,128,128]{2,1,0:T(8,128)(2,1)S(1)}, u32[]{:S(2)}, u32[]{:S(2)}) collective-permute-start(bf16[9,128,128]{2,1,0:T(8,128)(2,1)} %get-tuple-element.97), channel_id=1, source_target_pairs={{0,3},{1,4},{2,5},{3,6},{4,7},{5,0},{6,1},{7,2},{8,11},{9,12},{10,... | collective-permute-start | bytes 884744 | tf_op jit(solution)/shard_map/ppermute | solution.py:39
  12.7 0.2 collective-permute-start.6
  12.9 7.0 %collective-permute-done.2.rest_1_ = bf16[9,128,128]{2,1,0:T(8,128)(2,1)S(1)} collective-permute-done((bf16[9,128,128]{2,1,0:T(8,128)(2,1)S(1)}, bf16[9,128,128]{2,1,0:T(8,128)(2,1)S(1)}, u32[]{:S(2)}, u32[]{:S(2)}) %collective-permute-start.2) | collective-permute-done | bytes 294944 | tf_op jit(solution)/shard_map/ppermute | solution.py:39
  19.9 0.3 collective-permute-start.5
  20.1 2.8 %wanted.1 = (s32[24]{0:T(128)}, s32[128]{0:T(128)}, s32[128]{0:T(128)}) custom-call(s32[3,2,128]{2,1,0:T(2,128)} %bitcast.16), custom_call_target="tpu_custom_call" | custom-call | bytes 35000 | tf_op jit(solution)/shard_map/wanted/pallas_call | solution.py:199
  23.0 0.5 collective-permute-done.5.pos_r
  23.5 1.7 %collective-permute-start.4 = (s32[24]{0:T(128)}, s32[24]{0:T(128)S(1)}, u32[]{:S(2)}, u32[]{:S(2)}) collective-permute-start(s32[24]{0:T(128)} %get-tuple-element.76), channel_id=1, source_target_pairs={{0,8},{8,16},{16,24},{24,0},{1,9},{9,17},{17,25},{25,1},{2,10},{10... | collective-permute-start | bytes 296 | tf_op jit(solution)/shard_map/ppermute | solution.py:39
  25.2 1.1 %collective-permute-done.4.asked_r = s32[24]{0:T(128)S(1)} collective-permute-done((s32[24]{0:T(128)}, s32[24]{0:T(128)S(1)}, u32[]{:S(2)}, u32[]{:S(2)}) %collective-permute-start.4) | collective-permute-done | bytes 128 | tf_op jit(solution)/shard_map/ppermute | solution.py:39
  26.3 0.6 copy-done.12
  26.9 3.0 %places.1 = (s32[3,128]{1,0:T(4,128)}, s32[24]{0:T(128)}) custom-call(s32[3,2,128]{2,1,0:T(2,128)} %bitcast.17, s32[2]{0:T(128)} %bitcast.20, s32[128]{0:T(128)} %get-tuple-element.81.slots_l, s32[128]{0:T(128)} %get-tuple-element.82.slots_r, s32[63]{0:T(128)} %copy-done.6, s32[63]{0:T(128)} %copy-done.11, s32[24]{0:T(128)} %copy-done.12), custom_call_target="tpu_custom_call" | custom-call | tf_op jit(solution)/shard_map/places/pallas_call | solution.py:355
  29.9 1.2 %bitcast_convert_fusion.ids = s32[128]{0:T(128)} fusion(bf16[10,128,128]{2,1,0:T(8,128)(2,1)} %collective-permute-done.rest_3_), kind=kLoop, calls=%fused_computation | loop fusion | flops 128 | bytes 768 | tf_op jit(solution)/shard_map/convert_element_type | solution.py:451
  31.1 2.0 %asked.1.spots = s32[25]{0:T(128)} custom-call(s32[128]{0:T(128)} %bitcast_convert_fusion.ids, s32[63]{0:T(128)} %copy-done.6), custom_call_target="tpu_custom_call" | custom-call | tf_op jit(solution)/shard_map/asked/pallas_call | solution.py:233
  33.1 10.5 %collective-permute-done.6.rest_5_.rest_4_ = bf16[9,128,128]{2,1,0:T(8,128)(2,1)} collective-permute-done((bf16[9,128,128]{2,1,0:T(8,128)(2,1)}, bf16[9,128,128]{2,1,0:T(8,128)(2,1)}, u32[]{:S(2)}, u32[]{:S(2)}) %collective-permute-start.6) | collective-permute-done | bytes 294944 | tf_op jit(solution)/shard_map/ppermute | solution.py:39
  43.7 0.6 copy-done.8
  44.3 1.8 %pick_right.1 = bf16[24,128,128]{2,1,0:T(8,128)(2,1)S(1)} custom-call(s32[24]{0:T(128)S(1)} %copy-done.8, bf16[63,128,128]{2,1,0:T(8,128)(2,1)S(1)} %bitcast.13, bf16[9,128,128]{2,1,0:T(8,128)(2,1)S(1)} %collective-permute-done.3.rest_0_, bf16[9,128,128]{2,1,0:T(8,128)(2,1)S(1)} %collective-permute-done.2.rest_1_, ...), custom_call_target="tpu_custom_call" | custom-call | tf_op jit(solution)/shard_map/pick_right/pallas_call | solution.py:258
  46.1 0.0 copy-start.2
  46.1 0.0 copy-start.3
  46.1 0.3 collective-permute-start.10
  46.4 13.2 %collective-permute-done.8.rest_5_.rest_6_ = bf16[9,128,128]{2,1,0:T(8,128)(2,1)S(1)} collective-permute-done((bf16[9,128,128]{2,1,0:T(8,128)(2,1)}, bf16[9,128,128]{2,1,0:T(8,128)(2,1)S(1)}, u32[]{:S(2)}, u32[]{:S(2)}) %collective-permute-start.8) | collective-permute-done | bytes 294944 | tf_op jit(solution)/shard_map/ppermute | solution.py:39
  59.6 1.7 %pick_left.1 = bf16[24,128,128]{2,1,0:T(8,128)(2,1)S(1)} custom-call(s32[25]{0:T(128)S(1)} %copy-done.9, bf16[63,128,128]{2,1,0:T(8,128)(2,1)S(1)} %bitcast.14, bf16[9,128,128]{2,1,0:T(8,128)(2,1)S(1)} %collective-permute-done.3.rest_0_, bf16[9,128,128]{2,1,0:T(8,128)(2,1)S(1)} %collective-permute-done.2.rest_1_, ...), custom_call_target="tpu_custom_call" | custom-call | tf_op jit(solution)/shard_map/pick_left/pallas_call | solution.py:258
  61.3 0.3 collective-permute-start.9
  61.6 0.3 collective-permute-start.11
  61.9 4.5 %own_section.1.old = f32[33,128,128]{2,1,0:T(8,128)S(1)} custom-call(s32[3,2,128]{2,1,0:T(2,128)S(1)} %bitcast.19, s32[2]{0:T(128)S(1)} %bitcast.21, s32[63]{0:T(128)S(1)} %copy-done.7, bf16[63,128,128]{2,1,0:T(8,128)(2,1)S(1)} %bitcast.15, bf16[9,128,128]{2,1,0:T(8,128)(2,1)S(1)} %collective-permute-done.3.rest_0_, ...), custom_call_target="tpu_custom_call" | custom-call | bytes 35000 | tf_op jit(solution)/shard_map/own_section/pallas_call | solution.py:319
  66.4 5.3 %collective-permute-done.11.rest_0_ = bf16[9,128,128]{2,1,0:T(8,128)(2,1)S(1)} collective-permute-done((bf16[9,128,128]{2,1,0:T(8,128)(2,1)S(1)}, bf16[9,128,128]{2,1,0:T(8,128)(2,1)S(1)}, u32[]{:S(2)}, u32[]{:S(2)}) %collective-permute-start.11) | collective-permute-done | bytes 294944 | tf_op jit(solution)/shard_map/ppermute | solution.py:39
  71.6 3.0 %collective-permute-done.9.left = bf16[24,128,128]{2,1,0:T(8,128)(2,1)S(1)} collective-permute-done((bf16[24,128,128]{2,1,0:T(8,128)(2,1)S(1)}, bf16[24,128,128]{2,1,0:T(8,128)(2,1)S(1)}, u32[]{:S(2)}, u32[]{:S(2)}) %collective-permute-start.9) | collective-permute-done | bytes 786464 | tf_op jit(solution)/shard_map/ppermute | solution.py:39
  74.6 4.8 %next_section.1 = (f32[33,128,128]{2,1,0:T(8,128)S(1)}, bf16[32,128,128]{2,1,0:T(8,128)(2,1)}) custom-call(s32[1]{0:T(128)} %bitcast.1.col.token, s32[3,128]{1,0:T(4,128)S(1)} %copy-done.4, s32[2]{0:T(128)S(1)} %bitcast.22, f32[33,128,128]{2,1,0:T(8,128)S(1)} %own_section.1.old, ...), custom_call_target="tpu_custom_call", output_to_operand_aliasing={{0}: (3, {})} | custom-call | bytes 35000 | tf_op jit(solution)/shard_map/next_section/pallas_call | solution.py:397
  (28 shorter events, 0.1 us)
Async XLA Ops:
  0.0 2.8 %copy-start.5 = (s32[1,1,63]{2,1,0:T(1,128)S(1)}, s32[1,1,63]{2,1,0:T(1,128)}, u32[]{:S(2)}) copy-start(s32[1,1,63]{2,1,0:T(1,128)} %param.5) | copy-start | bytes 760
  0.0 2.8 %copy-start = (bf16[1,1,63,128,128]{4,3,2,1,0:T(8,128)(2,1)S(1)}, bf16[1,1,63,128,128]{4,3,2,1,0:T(8,128)(2,1)}, u32[]{:S(2)}) copy-start(bf16[1,1,63,128,128]{4,3,2,1,0:T(8,128)(2,1)} %param.4) | copy-start | bytes 6193156
  0.0 2.8 %copy-start.1 = (s32[1,1,2,128,3]{3,2,4,1,0:T(2,128)S(1)}, s32[1,1,2,128,3]{3,2,4,1,0:T(2,128)}, u32[]{:S(2)}) copy-start(s32[1,1,2,128,3]{3,2,4,1,0:T(2,128)} %param.6) | copy-start | bytes 9220
  2.7 9.9 %collective-permute-start.3 = (bf16[9,128,128]{2,1,0:T(8,128)(2,1)}, bf16[9,128,128]{2,1,0:T(8,128)(2,1)S(1)}, u32[]{:S(2)}, u32[]{:S(2)}) collective-permute-start(bf16[9,128,128]{2,1,0:T(8,128)(2,1)} %first_stage.1), channel_id=1, source_target_pairs={{0,2},{1,3},{2,4},{3,5},{4,6},{5,7},{6,0},{7,1},{8,10},{9,11},{10,... | collective-permute-start | bytes 884744 | tf_op jit(solution)/shard_map/ppermute | solution.py:39
  5.8 0.7 copy-start.10
  6.5 19.8 %copy-start.6 = (s32[63]{0:T(128)}, s32[63]{0:T(128)S(1)}, u32[]{:S(2)}) copy-start(s32[63]{0:T(128)S(1)} %get-tuple-element.77.pos) | copy-start | bytes 760
  6.5 23.4 %collective-permute-start = (bf16[10,128,128]{2,1,0:T(8,128)(2,1)}, bf16[10,128,128]{2,1,0:T(8,128)(2,1)}, u32[]{:S(2)}, u32[]{:S(2)}) collective-permute-start(bf16[10,128,128]{2,1,0:T(8,128)(2,1)} %get-tuple-element.64.self_ref), channel_id=1, source_target_pairs={{0,1},{1,2},{2,3},{3,4},{4,5},{5,6},{6,7},{7,0},{8,9},{9,10},{10,1... | collective-permute-start | bytes 983048 | tf_op jit(solution)/shard_map/ppermute | solution.py:39
  8.5 11.3 %collective-permute-start.2 = (bf16[9,128,128]{2,1,0:T(8,128)(2,1)S(1)}, bf16[9,128,128]{2,1,0:T(8,128)(2,1)S(1)}, u32[]{:S(2)}, u32[]{:S(2)}) collective-permute-start(bf16[9,128,128]{2,1,0:T(8,128)(2,1)S(1)} %get-tuple-element.66), channel_id=1, source_target_pairs={{0,7},{1,0},{2,1},{3,2},{4,3},{5,4},{6,5},{7,6},{8,15},{9,8},{10,9... | collective-permute-start | bytes 884744 | tf_op jit(solution)/shard_map/ppermute | solution.py:39
  8.6 21.3 %collective-permute-start.1 = (bf16[9,128,128]{2,1,0:T(8,128)(2,1)}, bf16[9,128,128]{2,1,0:T(8,128)(2,1)S(1)}, u32[]{:S(2)}, u32[]{:S(2)}) collective-permute-start(bf16[9,128,128]{2,1,0:T(8,128)(2,1)} %get-tuple-element.65), channel_id=1, source_target_pairs={{0,6},{1,7},{2,0},{3,1},{4,2},{5,3},{6,4},{7,5},{8,14},{9,15},{10,... | collective-permute-start | bytes 884744 | tf_op jit(solution)/shard_map/ppermute | solution.py:39
  8.9 24.2 %collective-permute-start.7 = (bf16[9,128,128]{2,1,0:T(8,128)(2,1)}, bf16[9,128,128]{2,1,0:T(8,128)(2,1)S(1)}, u32[]{:S(2)}, u32[]{:S(2)}) collective-permute-start(bf16[9,128,128]{2,1,0:T(8,128)(2,1)} %get-tuple-element.97), channel_id=1, source_target_pairs={{0,3},{1,4},{2,5},{3,6},{4,7},{5,0},{6,1},{7,2},{8,11},{9,12},{10,... | collective-permute-start | bytes 884744 | tf_op jit(solution)/shard_map/ppermute | solution.py:39
  12.7 31.0 %collective-permute-start.6 = (bf16[9,128,128]{2,1,0:T(8,128)(2,1)}, bf16[9,128,128]{2,1,0:T(8,128)(2,1)}, u32[]{:S(2)}, u32[]{:S(2)}) collective-permute-start(bf16[9,128,128]{2,1,0:T(8,128)(2,1)} %get-tuple-element.96), channel_id=1, source_target_pairs={{0,5},{1,6},{2,7},{3,0},{4,1},{5,2},{6,3},{7,4},{8,13},{9,14},{10,... | collective-permute-start | bytes 884744 | tf_op jit(solution)/shard_map/ppermute | solution.py:39
  19.9 3.6 %collective-permute-start.5 = (s32[63]{0:T(128)S(1)}, s32[63]{0:T(128)S(1)}, u32[]{:S(2)}, u32[]{:S(2)}) collective-permute-start(s32[63]{0:T(128)S(1)} %get-tuple-element.77.pos), channel_id=1, source_target_pairs={{0,24},{8,0},{16,8},{24,16},{1,25},{9,1},{17,9},{25,17},{2,26},{10... | collective-permute-start | bytes 764 | tf_op jit(solution)/shard_map/ppermute | solution.py:39
  23.5 2.9 %copy-start.11 = (s32[63]{0:T(128)}, s32[63]{0:T(128)S(1)}, u32[]{:S(2)}) copy-start(s32[63]{0:T(128)S(1)} %collective-permute-done.5.pos_r) | copy-start | bytes 760
  23.5 2.8 %collective-permute-start.4 = (s32[24]{0:T(128)}, s32[24]{0:T(128)S(1)}, u32[]{:S(2)}, u32[]{:S(2)}) collective-permute-start(s32[24]{0:T(128)} %get-tuple-element.76), channel_id=1, source_target_pairs={{0,8},{8,16},{16,24},{24,0},{1,9},{9,17},{17,25},{25,1},{2,10},{10... | collective-permute-start | bytes 296 | tf_op jit(solution)/shard_map/ppermute | solution.py:39
  26.3 0.6 copy-start.12
  43.7 16.0 %collective-permute-start.8 = (bf16[9,128,128]{2,1,0:T(8,128)(2,1)}, bf16[9,128,128]{2,1,0:T(8,128)(2,1)S(1)}, u32[]{:S(2)}, u32[]{:S(2)}) collective-permute-start(bf16[9,128,128]{2,1,0:T(8,128)(2,1)} %copy-done.10), channel_id=1, source_target_pairs={{0,4},{1,5},{2,6},{3,7},{4,0},{5,1},{6,2},{7,3},{8,12},{9,13},{10,... | collective-permute-start | bytes 884744 | tf_op jit(solution)/shard_map/ppermute | solution.py:39
  43.7 0.6 copy-start.8
  44.3 15.4 %copy-start.9 = (s32[25]{0:T(128)S(1)}, s32[25]{0:T(128)}, u32[]{:S(2)}) copy-start(s32[25]{0:T(128)} %asked.1.spots) | copy-start | bytes 304
  46.1 15.8 %copy-start.2 = (s32[1,1,2,128,3]{3,2,4,1,0:T(2,128)S(1)}, s32[1,1,2,128,3]{3,2,4,1,0:T(2,128)}, u32[]{:S(2)}) copy-start(s32[1,1,2,128,3]{3,2,4,1,0:T(2,128)} %param.6) | copy-start | bytes 9220
  46.1 15.8 %copy-start.3 = (s32[1,1,2]{2,1,0:T(1,128)S(1)}, s32[1,1,2]{2,1,0:T(1,128)}, u32[]{:S(2)}) copy-start(s32[1,1,2]{2,1,0:T(1,128)} %param.7) | copy-start | bytes 28
  46.1 15.8 %copy-start.7 = (s32[63]{0:T(128)S(1)}, s32[63]{0:T(128)}, u32[]{:S(2)}) copy-start(s32[63]{0:T(128)} %copy-done.6) | copy-start | bytes 760
  46.1 25.5 %collective-permute-start.10 = (bf16[24,128,128]{2,1,0:T(8,128)(2,1)S(1)}, bf16[24,128,128]{2,1,0:T(8,128)(2,1)S(1)}, u32[]{:S(2)}, u32[]{:S(2)}) collective-permute-start(bf16[24,128,128]{2,1,0:T(8,128)(2,1)S(1)} %pick_right.1), channel_id=1, source_target_pairs={{0,24},{8,0},{16,8},{24,16},{1,25},{9,1},{17,9},{25,17},{2,26},{10... | collective-permute-start | bytes 2359304 | tf_op jit(solution)/shard_map/ppermute | solution.py:39
  61.3 13.3 %copy-start.4 = (s32[3,128]{1,0:T(4,128)S(1)}, s32[3,128]{1,0:T(4,128)}, u32[]{:S(2)}) copy-start(s32[3,128]{1,0:T(4,128)} %get-tuple-element.115.spots) | copy-start | bytes 4612
  61.3 13.3 %collective-permute-start.9 = (bf16[24,128,128]{2,1,0:T(8,128)(2,1)S(1)}, bf16[24,128,128]{2,1,0:T(8,128)(2,1)S(1)}, u32[]{:S(2)}, u32[]{:S(2)}) collective-permute-start(bf16[24,128,128]{2,1,0:T(8,128)(2,1)S(1)} %pick_left.1), channel_id=1, source_target_pairs={{0,7},{1,0},{2,1},{3,2},{4,3},{5,4},{6,5},{7,6},{8,15},{9,8},{10,9... | collective-permute-start | bytes 2359304 | tf_op jit(solution)/shard_map/ppermute | solution.py:39
  61.6 10.0 %collective-permute-start.11 = (bf16[9,128,128]{2,1,0:T(8,128)(2,1)S(1)}, bf16[9,128,128]{2,1,0:T(8,128)(2,1)S(1)}, u32[]{:S(2)}, u32[]{:S(2)}) collective-permute-start(bf16[9,128,128]{2,1,0:T(8,128)(2,1)S(1)} %collective-permute-done.8.rest_5_.rest_6_), channel_id=1, source_target_pairs={{0,24},{8,0},{16,8},{24,16},{1,25},{9,1},{17,9},{25,17},{2,26},{10... | collective-permute-start | bytes 884744 | tf_op jit(solution)/shard_map/ppermute | solution.py:39
where the time goes:
time: 79.7 us; the launch traced here: 79.4 us
  waiting for transfers between devices  40.6 us (51%)
  Pallas kernels  26.3 us (33%)
  starting transfers between devices  9.27 us (12%)
  local copies, waits for them, and re-layouts  1.95 us (2%)
  other arithmetic  1.18 us (1%)
    ppermute x12, waiting for transfers between devices, moved(): lax.ppermute(value, axis, [(s, (s + steps) % count) for s in range(count)])  40.6 us
    ppermute x12, starting transfers between devices, moved(): lax.ppermute(value, axis, [(s, (s + steps) % count) for s in range(count)])  9.27 us
    pallas_call x1, Pallas kernels, next_section(): pl.pallas_call(functools.partial(next_kernel, lay, late), out_shape=(jax....  4.79 us
    pallas_call x1, Pallas kernels, own_section(): pl.pallas_call(functools.partial(own_kernel, lay, prods), out_shape=jax.S...  4.46 us
    pallas_call x2, Pallas kernels, pick(): pl.pallas_call(functools.partial(pick_kernel, lay, stages, pieces), out_s...  3.5 us
    pallas_call x1, Pallas kernels, places(): pl.pallas_call(functools.partial(places_kernel, lay, late), out_shape=(i3...  3 us
    pallas_call x1, Pallas kernels, rest_stages(): pl.pallas_call(functools.partial(rest_kernel, lay), out_shape=shapes + (i...  2.93 us
    pallas_call x1, Pallas kernels, wanted(): pl.pallas_call(functools.partial(wanted_kernel, prods), out_shape=(i32(US...  2.85 us
  transfers between devices with their start and end apart: 12, of which 7 were waited for; matrix products, arithmetic and copies ran while one was open for 1% of the time, Pallas kernels for 24%

commit v1 on v0

--- a/solution.py
+++ b/solution.py
@@ -64,7 +64,7 @@
         pieces = min(5, len(others))
         cuts = [len(others) * i // pieces for i in range(pieces + 1)]
         groups = [others[a:b] for a, b in zip(cuts, cuts[1:])]
-        self.stages = groups[:3] + [[1]] + groups[3:] + [[half]]
+        self.stages = groups[:1] + [[1]] + groups[1:] + [[half]]
         self.base = [0] * cols
         self.start = []
         at = 0
@@ -371,7 +371,9 @@
 
 
 def next_kernel(lay, late, token, spots, counts, old, self_ref, left, right, *rest):
-    parts, (acc, out) = rest[:-2], rest[-2:]
+    parts, (out, acc) = rest[:-2], rest[-2:]
+    for o in range(OUTSLOTS + 1):
+        acc[o] = old[o]
     lefts = [(self_ref, lay.size(lay.self_stage))]
     rights = [(part, lay.size(s)) for s, part in zip(late, parts)]
 
@@ -396,17 +398,14 @@
     block = self_part.shape[-1]
     return pl.pallas_call(
         functools.partial(next_kernel, lay, late),
-        out_shape=(
-            jax.ShapeDtypeStruct(acc.shape, acc.dtype),
-            jax.ShapeDtypeStruct((OUTSLOTS, block, block), self_part.dtype),
-        ),
+        out_shape=jax.ShapeDtypeStruct((OUTSLOTS, block, block), self_part.dtype),
         in_specs=[SMEM] * 3 + [VMEM] * (4 + len(parts)),
-        out_specs=(VMEM, VMEM),
-        input_output_aliases={3: 0},
+        out_specs=VMEM,
+        scratch_shapes=[pltpu.VMEM(acc.shape, acc.dtype)],
         compiler_params=params(20),
         cost_estimate=cost(0.01),
         name="next_section",
-    )(token, spots, counts, acc, self_part, left, right, *parts)[1]
+    )(token, spots, counts, acc, self_part, left, right, *parts)
 
 
 FLIGHT = 2

time: 79.7 us -> 79.8 us (level); the launches traced: 79.4 us -> 78.6 us
  Pallas kernels: 26.3 us -> 24.2 us
  starting transfers between devices: 9.27 us -> 10.2 us
    pallas_call x1, Pallas kernels: 4.46 us -> 3.17 us  [own_section(): pl.pallas_call(functools.partial(own_kernel, lay, prods), out_shape=jax.S...]
    ppermute x12, starting transfers between devices: 9.27 us -> 10.2 us  [moved(): lax.ppermute(value, axis, [(s, (s + steps) % count) for s in range(count)])]
    unnamed x26 -> x30, local copies, waits for them, and re-layouts: 1.95 us -> 2.01 us
  transfers between devices with their start and end apart: 12 -> 12, of which waited for: 7 -> 7; matrix products, arithmetic and copies ran while one was open for 1% -> 2% of each run, Pallas kernels for 24% -> 22%
where the time goes in v1:
time: 79.8 us; the launch traced here: 78.6 us
  waiting for transfers between devices  40.8 us (51%)
  Pallas kernels  24.2 us (30%)
  starting transfers between devices  10.2 us (13%)
  local copies, waits for them, and re-layouts  2.01 us (3%)
  other arithmetic  1.18 us (1%)
    ppermute x12, waiting for transfers between devices, moved(): lax.ppermute(value, axis, [(s, (s + steps) % count) for s in range(count)])  40.8 us
    ppermute x12, starting transfers between devices, moved(): lax.ppermute(value, axis, [(s, (s + steps) % count) for s in range(count)])  10.2 us
    pallas_call x1, Pallas kernels, next_section(): pl.pallas_call(functools.partial(next_kernel, lay, late), out_shape=jax.S...  4.03 us
    pallas_call x2, Pallas kernels, pick(): pl.pallas_call(functools.partial(pick_kernel, lay, stages, pieces), out_s...  3.5 us
    pallas_call x1, Pallas kernels, own_section(): pl.pallas_call(functools.partial(own_kernel, lay, prods), out_shape=jax.S...  3.17 us
    pallas_call x1, Pallas kernels, places(): pl.pallas_call(functools.partial(places_kernel, lay, late), out_shape=(i3...  3 us
    pallas_call x1, Pallas kernels, rest_stages(): pl.pallas_call(functools.partial(rest_kernel, lay), out_shape=shapes + (i...  2.96 us
    pallas_call x1, Pallas kernels, wanted(): pl.pallas_call(functools.partial(wanted_kernel, prods), out_shape=(i32(US...  2.85 us
  transfers between devices with their start and end apart: 12, of which 7 were waited for; matrix products, arithmetic and copies ran while one was open for 2% of the time, Pallas kernels for 22%

profile of v1, /device:TPU:31, one launch (start us, length us, event | category | flops | bytes accessed | tf_op | source)
XLA Modules:
  0.0 78.6 jit_solution(5199774600083269656)
XLA Ops:
  0.0 2.7 %first_stage.1 = bf16[9,128,128]{2,1,0:T(8,128)(2,1)} custom-call(s32[63]{0:T(128)} %bitcast.23, s32[1]{0:T(128)} %bitcast.1.col.token, bf16[63,128,128]{2,1,0:T(8,128)(2,1)} %bitcast.11), custom_call_target="tpu_custom_call" | custom-call | tf_op jit(solution)/shard_map/first_stage/pallas_call | solution.py:113
  2.7 0.1 collective-permute-start.1
  2.8 3.0 %rest_stages.1 = (bf16[10,128,128]{2,1,0:T(8,128)(2,1)S(1)}, bf16[9,128,128]{2,1,0:T(8,128)(2,1)}, bf16[9,128,128]{2,1,0:T(8,128)(2,1)}, bf16[9,128,128]{2,1,0:T...) custom-call(s32[63]{0:T(128)S(1)} %bitcast.24, s32[1]{0:T(128)} %bitcast.1.col.token, ...), custom_call_target="tpu_custom_call" | custom-call | bytes 35000 | tf_op jit(solution)/shard_map/rest_stages/pallas_call | solution.py:162
  5.8 2.1 %collective-permute-start = (bf16[10,128,128]{2,1,0:T(8,128)(2,1)S(1)}, bf16[10,128,128]{2,1,0:T(8,128)(2,1)}, u32[]{:S(2)}, u32[]{:S(2)}) collective-permute-start(bf16[10,128,128]{2,1,0:T(8,128)(2,1)S(1)} %get-tuple-element.63.self_ref), channel_id=1, source_target_pairs={{0,1},{1,2},{2,3},{3,4},{4,5},{5,6},{6,7},{7,0},{8,9},{9,10},{10,1... | collective-permute-start | bytes 983048 | tf_op jit(solution)/shard_map/ppermute | solution.py:39
  7.9 0.7 copy-done.1
  8.6 1.0 %collective-permute-start.2 = (bf16[9,128,128]{2,1,0:T(8,128)(2,1)}, bf16[9,128,128]{2,1,0:T(8,128)(2,1)S(1)}, u32[]{:S(2)}, u32[]{:S(2)}) collective-permute-start(bf16[9,128,128]{2,1,0:T(8,128)(2,1)} %get-tuple-element.68), channel_id=1, source_target_pairs={{0,6},{1,7},{2,0},{3,1},{4,2},{5,3},{6,4},{7,5},{8,14},{9,15},{10,... | collective-permute-start | bytes 884744 | tf_op jit(solution)/shard_map/ppermute | solution.py:39
  9.6 3.1 %collective-permute-start.7 = (bf16[9,128,128]{2,1,0:T(8,128)(2,1)}, bf16[9,128,128]{2,1,0:T(8,128)(2,1)S(1)}, u32[]{:S(2)}, u32[]{:S(2)}) collective-permute-start(bf16[9,128,128]{2,1,0:T(8,128)(2,1)} %get-tuple-element.96), channel_id=1, source_target_pairs={{0,3},{1,4},{2,5},{3,6},{4,7},{5,0},{6,1},{7,2},{8,11},{9,12},{10,... | collective-permute-start | bytes 884744 | tf_op jit(solution)/shard_map/ppermute | solution.py:39
  12.7 0.9 %collective-permute-start.6 = (bf16[9,128,128]{2,1,0:T(8,128)(2,1)}, bf16[9,128,128]{2,1,0:T(8,128)(2,1)}, u32[]{:S(2)}, u32[]{:S(2)}) collective-permute-start(bf16[9,128,128]{2,1,0:T(8,128)(2,1)} %get-tuple-element.95), channel_id=1, source_target_pairs={{0,5},{1,6},{2,7},{3,0},{4,1},{5,2},{6,3},{7,4},{8,13},{9,14},{10,... | collective-permute-start | bytes 884744 | tf_op jit(solution)/shard_map/ppermute | solution.py:39
  13.6 2.1 %collective-permute-done.rest_1_ = bf16[10,128,128]{2,1,0:T(8,128)(2,1)} collective-permute-done((bf16[10,128,128]{2,1,0:T(8,128)(2,1)S(1)}, bf16[10,128,128]{2,1,0:T(8,128)(2,1)}, u32[]{:S(2)}, u32[]{:S(2)}) %collective-permute-start) | collective-permute-done | bytes 327712 | tf_op jit(solution)/shard_map/ppermute | solution.py:39
  15.8 0.3 collective-permute-start.5
  16.0 2.8 %wanted.1 = (s32[24]{0:T(128)}, s32[128]{0:T(128)}, s32[128]{0:T(128)}) custom-call(s32[3,2,128]{2,1,0:T(2,128)} %bitcast.16), custom_call_target="tpu_custom_call" | custom-call | bytes 35000 | tf_op jit(solution)/shard_map/wanted/pallas_call | solution.py:199
  18.9 0.2 collective-permute-done.5.pos_r
  19.1 2.0 %collective-permute-start.4 = (s32[24]{0:T(128)}, s32[24]{0:T(128)S(1)}, u32[]{:S(2)}, u32[]{:S(2)}) collective-permute-start(s32[24]{0:T(128)} %get-tuple-element.76), channel_id=1, source_target_pairs={{0,8},{8,16},{16,24},{24,0},{1,9},{9,17},{17,25},{25,1},{2,10},{10... | collective-permute-start | bytes 296 | tf_op jit(solution)/shard_map/ppermute | solution.py:39
  21.1 1.2 %bitcast_convert_fusion.ids = s32[128]{0:T(128)} fusion(bf16[10,128,128]{2,1,0:T(8,128)(2,1)} %collective-permute-done.rest_1_), kind=kLoop, calls=%fused_computation | loop fusion | flops 128 | bytes 768 | tf_op jit(solution)/shard_map/convert_element_type | solution.py:450
  22.3 0.6 copy-done.14
  22.8 3.0 %places.1 = (s32[3,128]{1,0:T(4,128)}, s32[24]{0:T(128)}) custom-call(s32[3,2,128]{2,1,0:T(2,128)} %bitcast.17, s32[2]{0:T(128)} %bitcast.20, s32[128]{0:T(128)} %get-tuple-element.81.slots_l, s32[128]{0:T(128)} %get-tuple-element.82.slots_r, s32[63]{0:T(128)} %copy-done.8, s32[63]{0:T(128)} %copy-done.13, s32[24]{0:T(128)} %copy-done.14), custom_call_target="tpu_custom_call" | custom-call | tf_op jit(solution)/shard_map/places/pallas_call | solution.py:355
  25.8 2.0 %asked.1.spots = s32[25]{0:T(128)} custom-call(s32[128]{0:T(128)} %bitcast_convert_fusion.ids, s32[63]{0:T(128)} %copy-done.8), custom_call_target="tpu_custom_call" | custom-call | tf_op jit(solution)/shard_map/asked/pallas_call | solution.py:233
  27.9 0.7 collective-permute-done.7.rest_4_.rest_3_
  28.6 15.1 %collective-permute-done.6.rest_5_.rest_4_ = bf16[9,128,128]{2,1,0:T(8,128)(2,1)} collective-permute-done((bf16[9,128,128]{2,1,0:T(8,128)(2,1)}, bf16[9,128,128]{2,1,0:T(8,128)(2,1)}, u32[]{:S(2)}, u32[]{:S(2)}) %collective-permute-start.6) | collective-permute-done | bytes 294944 | tf_op jit(solution)/shard_map/ppermute | solution.py:39
  43.7 0.7 copy-done.10
  44.3 1.8 %pick_right.1 = bf16[24,128,128]{2,1,0:T(8,128)(2,1)S(1)} custom-call(s32[24]{0:T(128)S(1)} %copy-done.10, bf16[63,128,128]{2,1,0:T(8,128)(2,1)S(1)} %bitcast.13, bf16[9,128,128]{2,1,0:T(8,128)(2,1)S(1)} %collective-permute-done.1.rest_0_, bf16[10,128,128]{2,1,0:T(8,128)(2,1)} %collective-permute-done.rest_1_, ...), custom_call_target="tpu_custom_call" | custom-call | tf_op jit(solution)/shard_map/pick_right/pallas_call | solution.py:258
  46.2 0.0 copy-start.5
  46.2 0.3 collective-permute-start.10
  46.5 13.1 %collective-permute-done.8.rest_5_.rest_6_ = bf16[9,128,128]{2,1,0:T(8,128)(2,1)S(1)} collective-permute-done((bf16[9,128,128]{2,1,0:T(8,128)(2,1)}, bf16[9,128,128]{2,1,0:T(8,128)(2,1)S(1)}, u32[]{:S(2)}, u32[]{:S(2)}) %collective-permute-start.8) | collective-permute-done | bytes 294944 | tf_op jit(solution)/shard_map/ppermute | solution.py:39
  59.6 1.7 %pick_left.1 = bf16[24,128,128]{2,1,0:T(8,128)(2,1)S(1)} custom-call(s32[25]{0:T(128)S(1)} %copy-done.11, bf16[63,128,128]{2,1,0:T(8,128)(2,1)S(1)} %bitcast.14, bf16[9,128,128]{2,1,0:T(8,128)(2,1)S(1)} %collective-permute-done.1.rest_0_, bf16[9,128,128]{2,1,0:T(8,128)(2,1)S(1)} %collective-permute-done.3.rest_2_.rest_1_, ...), custom_call_target="tpu_custom_call" | custom-call | tf_op jit(solution)/shard_map/pick_left/pallas_call | solution.py:258
  61.3 0.0 copy-start.2
  61.3 0.3 collective-permute-start.9
  61.6 0.3 collective-permute-start.11
  61.9 3.2 %own_section.1.old = f32[33,128,128]{2,1,0:T(8,128)S(1)} custom-call(s32[3,2,128]{2,1,0:T(2,128)S(1)} %bitcast.19, s32[2]{0:T(128)S(1)} %bitcast.21, s32[63]{0:T(128)S(1)} %copy-done.9, bf16[63,128,128]{2,1,0:T(8,128)(2,1)S(1)} %bitcast.15, bf16[9,128,128]{2,1,0:T(8,128)(2,1)S(1)} %collective-permute-done.1.rest_0_, ...), custom_call_target="tpu_custom_call" | custom-call | bytes 35000 | tf_op jit(solution)/shard_map/own_section/pallas_call | solution.py:319
  65.0 6.6 %collective-permute-done.11.rest_0_ = bf16[9,128,128]{2,1,0:T(8,128)(2,1)S(1)} collective-permute-done((bf16[9,128,128]{2,1,0:T(8,128)(2,1)S(1)}, bf16[9,128,128]{2,1,0:T(8,128)(2,1)S(1)}, u32[]{:S(2)}, u32[]{:S(2)}) %collective-permute-start.11) | collective-permute-done | bytes 294944 | tf_op jit(solution)/shard_map/ppermute | solution.py:39
  71.6 3.0 %collective-permute-done.9.left = bf16[24,128,128]{2,1,0:T(8,128)(2,1)S(1)} collective-permute-done((bf16[24,128,128]{2,1,0:T(8,128)(2,1)S(1)}, bf16[24,128,128]{2,1,0:T(8,128)(2,1)S(1)}, u32[]{:S(2)}, u32[]{:S(2)}) %collective-permute-start.9) | collective-permute-done | bytes 786464 | tf_op jit(solution)/shard_map/ppermute | solution.py:39
  74.6 4.0 %next_section.1 = bf16[32,128,128]{2,1,0:T(8,128)(2,1)} custom-call(s32[1]{0:T(128)} %bitcast.1.col.token, s32[3,128]{1,0:T(4,128)S(1)} %copy-done.6, s32[2]{0:T(128)S(1)} %bitcast.22, f32[33,128,128]{2,1,0:T(8,128)S(1)} %own_section.1.old, bf16[10,128,128]{2,1,0:T(8,128)(2,1)S(1)} %copy-done.2, bf16[24,128,128]{2,1,0:T(8,128)(2,1)S(1)} %collective-permute-done.9.left, ...), custom_call_target="tpu_custom_call" | custom-call | bytes 35000 | tf_op jit(solution)/shard_map/next_section/pallas_call | solution.py:399
  (32 shorter events, 0.1 us)
Async XLA Ops:
  0.0 2.8 %copy-start = (bf16[1,1,63,128,128]{4,3,2,1,0:T(8,128)(2,1)S(1)}, bf16[1,1,63,128,128]{4,3,2,1,0:T(8,128)(2,1)}, u32[]{:S(2)}) copy-start(bf16[1,1,63,128,128]{4,3,2,1,0:T(8,128)(2,1)} %param.4) | copy-start | bytes 6193156
  0.0 2.8 %copy-start.7 = (s32[1,1,63]{2,1,0:T(1,128)S(1)}, s32[1,1,63]{2,1,0:T(1,128)}, u32[]{:S(2)}) copy-start(s32[1,1,63]{2,1,0:T(1,128)} %param.5) | copy-start | bytes 760
  0.0 2.8 %copy-start.3 = (s32[1,1,2,128,3]{3,2,4,1,0:T(2,128)S(1)}, s32[1,1,2,128,3]{3,2,4,1,0:T(2,128)}, u32[]{:S(2)}) copy-start(s32[1,1,2,128,3]{3,2,4,1,0:T(2,128)} %param.6) | copy-start | bytes 9220
  2.7 10.0 %collective-permute-start.1 = (bf16[9,128,128]{2,1,0:T(8,128)(2,1)}, bf16[9,128,128]{2,1,0:T(8,128)(2,1)S(1)}, u32[]{:S(2)}, u32[]{:S(2)}) collective-permute-start(bf16[9,128,128]{2,1,0:T(8,128)(2,1)} %first_stage.1), channel_id=1, source_target_pairs={{0,2},{1,3},{2,4},{3,5},{4,6},{5,7},{6,0},{7,1},{8,10},{9,11},{10,... | collective-permute-start | bytes 884744 | tf_op jit(solution)/shard_map/ppermute | solution.py:39
  5.8 2.1 %copy-start.12 = (bf16[9,128,128]{2,1,0:T(8,128)(2,1)}, bf16[9,128,128]{2,1,0:T(8,128)(2,1)S(1)}, u32[]{:S(2)}) copy-start(bf16[9,128,128]{2,1,0:T(8,128)(2,1)S(1)} %get-tuple-element.100) | copy-start | bytes 884740
  5.8 16.5 %copy-start.8 = (s32[63]{0:T(128)}, s32[63]{0:T(128)S(1)}, u32[]{:S(2)}) copy-start(s32[63]{0:T(128)S(1)} %get-tuple-element.77.pos) | copy-start | bytes 760
  5.8 10.0 %collective-permute-start = (bf16[10,128,128]{2,1,0:T(8,128)(2,1)S(1)}, bf16[10,128,128]{2,1,0:T(8,128)(2,1)}, u32[]{:S(2)}, u32[]{:S(2)}) collective-permute-start(bf16[10,128,128]{2,1,0:T(8,128)(2,1)S(1)} %get-tuple-element.63.self_ref), channel_id=1, source_target_pairs={{0,1},{1,2},{2,3},{3,4},{4,5},{5,6},{6,7},{7,0},{8,9},{9,10},{10,1... | collective-permute-start | bytes 983048 | tf_op jit(solution)/shard_map/ppermute | solution.py:39
  7.9 0.7 copy-start.1
  8.6 17.2 %collective-permute-start.3 = (bf16[9,128,128]{2,1,0:T(8,128)(2,1)}, bf16[9,128,128]{2,1,0:T(8,128)(2,1)S(1)}, u32[]{:S(2)}, u32[]{:S(2)}) collective-permute-start(bf16[9,128,128]{2,1,0:T(8,128)(2,1)} %get-tuple-element.69), channel_id=1, source_target_pairs={{0,7},{1,0},{2,1},{3,2},{4,3},{5,4},{6,5},{7,6},{8,15},{9,8},{10,9... | collective-permute-start | bytes 884744 | tf_op jit(solution)/shard_map/ppermute | solution.py:39
  8.6 17.2 %collective-permute-start.2 = (bf16[9,128,128]{2,1,0:T(8,128)(2,1)}, bf16[9,128,128]{2,1,0:T(8,128)(2,1)S(1)}, u32[]{:S(2)}, u32[]{:S(2)}) collective-permute-start(bf16[9,128,128]{2,1,0:T(8,128)(2,1)} %get-tuple-element.68), channel_id=1, source_target_pairs={{0,6},{1,7},{2,0},{3,1},{4,2},{5,3},{6,4},{7,5},{8,14},{9,15},{10,... | collective-permute-start | bytes 884744 | tf_op jit(solution)/shard_map/ppermute | solution.py:39
  9.6 19.0 %collective-permute-start.7 = (bf16[9,128,128]{2,1,0:T(8,128)(2,1)}, bf16[9,128,128]{2,1,0:T(8,128)(2,1)S(1)}, u32[]{:S(2)}, u32[]{:S(2)}) collective-permute-start(bf16[9,128,128]{2,1,0:T(8,128)(2,1)} %get-tuple-element.96), channel_id=1, source_target_pairs={{0,3},{1,4},{2,5},{3,6},{4,7},{5,0},{6,1},{7,2},{8,11},{9,12},{10,... | collective-permute-start | bytes 884744 | tf_op jit(solution)/shard_map/ppermute | solution.py:39
  12.7 30.9 %collective-permute-start.6 = (bf16[9,128,128]{2,1,0:T(8,128)(2,1)}, bf16[9,128,128]{2,1,0:T(8,128)(2,1)}, u32[]{:S(2)}, u32[]{:S(2)}) collective-permute-start(bf16[9,128,128]{2,1,0:T(8,128)(2,1)} %get-tuple-element.95), channel_id=1, source_target_pairs={{0,5},{1,6},{2,7},{3,0},{4,1},{5,2},{6,3},{7,4},{8,13},{9,14},{10,... | collective-permute-start | bytes 884744 | tf_op jit(solution)/shard_map/ppermute | solution.py:39
  15.8 3.3 %collective-permute-start.5 = (s32[63]{0:T(128)S(1)}, s32[63]{0:T(128)S(1)}, u32[]{:S(2)}, u32[]{:S(2)}) collective-permute-start(s32[63]{0:T(128)S(1)} %get-tuple-element.77.pos), channel_id=1, source_target_pairs={{0,24},{8,0},{16,8},{24,16},{1,25},{9,1},{17,9},{25,17},{2,26},{10... | collective-permute-start | bytes 764 | tf_op jit(solution)/shard_map/ppermute | solution.py:39
  19.1 3.2 %copy-start.13 = (s32[63]{0:T(128)}, s32[63]{0:T(128)S(1)}, u32[]{:S(2)}) copy-start(s32[63]{0:T(128)S(1)} %collective-permute-done.5.pos_r) | copy-start | bytes 760
  19.1 3.2 %collective-permute-start.4 = (s32[24]{0:T(128)}, s32[24]{0:T(128)S(1)}, u32[]{:S(2)}, u32[]{:S(2)}) collective-permute-start(s32[24]{0:T(128)} %get-tuple-element.76), channel_id=1, source_target_pairs={{0,8},{8,16},{16,24},{24,0},{1,9},{9,17},{17,25},{25,1},{2,10},{10... | collective-permute-start | bytes 296 | tf_op jit(solution)/shard_map/ppermute | solution.py:39
  22.2 0.6 copy-start.14
  43.7 15.9 %collective-permute-start.8 = (bf16[9,128,128]{2,1,0:T(8,128)(2,1)}, bf16[9,128,128]{2,1,0:T(8,128)(2,1)S(1)}, u32[]{:S(2)}, u32[]{:S(2)}) collective-permute-start(bf16[9,128,128]{2,1,0:T(8,128)(2,1)} %copy-done.12), channel_id=1, source_target_pairs={{0,4},{1,5},{2,6},{3,7},{4,0},{5,1},{6,2},{7,3},{8,12},{9,13},{10,... | collective-permute-start | bytes 884744 | tf_op jit(solution)/shard_map/ppermute | solution.py:39
  43.7 0.7 copy-start.10
  44.3 15.3 %copy-start.11 = (s32[25]{0:T(128)S(1)}, s32[25]{0:T(128)}, u32[]{:S(2)}) copy-start(s32[25]{0:T(128)} %asked.1.spots) | copy-start | bytes 304
  46.2 15.7 %copy-start.4 = (s32[1,1,2,128,3]{3,2,4,1,0:T(2,128)S(1)}, s32[1,1,2,128,3]{3,2,4,1,0:T(2,128)}, u32[]{:S(2)}) copy-start(s32[1,1,2,128,3]{3,2,4,1,0:T(2,128)} %param.6) | copy-start | bytes 9220
  46.2 15.7 %copy-start.5 = (s32[1,1,2]{2,1,0:T(1,128)S(1)}, s32[1,1,2]{2,1,0:T(1,128)}, u32[]{:S(2)}) copy-start(s32[1,1,2]{2,1,0:T(1,128)} %param.7) | copy-start | bytes 28
  46.2 15.7 %copy-start.9 = (s32[63]{0:T(128)S(1)}, s32[63]{0:T(128)}, u32[]{:S(2)}) copy-start(s32[63]{0:T(128)} %copy-done.8) | copy-start | bytes 760
  46.2 25.4 %collective-permute-start.10 = (bf16[24,128,128]{2,1,0:T(8,128)(2,1)S(1)}, bf16[24,128,128]{2,1,0:T(8,128)(2,1)S(1)}, u32[]{:S(2)}, u32[]{:S(2)}) collective-permute-start(bf16[24,128,128]{2,1,0:T(8,128)(2,1)S(1)} %pick_right.1), channel_id=1, source_target_pairs={{0,24},{8,0},{16,8},{24,16},{1,25},{9,1},{17,9},{25,17},{2,26},{10... | collective-permute-start | bytes 2359304 | tf_op jit(solution)/shard_map/ppermute | solution.py:39
  61.3 13.3 %copy-start.2 = (bf16[10,128,128]{2,1,0:T(8,128)(2,1)S(1)}, bf16[10,128,128]{2,1,0:T(8,128)(2,1)}, u32[]{:S(2)}) copy-start(bf16[10,128,128]{2,1,0:T(8,128)(2,1)} %copy-done.1) | copy-start | bytes 983044
  61.3 13.3 %copy-start.6 = (s32[3,128]{1,0:T(4,128)S(1)}, s32[3,128]{1,0:T(4,128)}, u32[]{:S(2)}) copy-start(s32[3,128]{1,0:T(4,128)} %get-tuple-element.114.spots) | copy-start | bytes 4612
  61.3 13.3 %collective-permute-start.9 = (bf16[24,128,128]{2,1,0:T(8,128)(2,1)S(1)}, bf16[24,128,128]{2,1,0:T(8,128)(2,1)S(1)}, u32[]{:S(2)}, u32[]{:S(2)}) collective-permute-start(bf16[24,128,128]{2,1,0:T(8,128)(2,1)S(1)} %pick_left.1), channel_id=1, source_target_pairs={{0,7},{1,0},{2,1},{3,2},{4,3},{5,4},{6,5},{7,6},{8,15},{9,8},{10,9... | collective-permute-start | bytes 2359304 | tf_op jit(solution)/shard_map/ppermute | solution.py:39
  61.6 10.0 %collective-permute-start.11 = (bf16[9,128,128]{2,1,0:T(8,128)(2,1)S(1)}, bf16[9,128,128]{2,1,0:T(8,128)(2,1)S(1)}, u32[]{:S(2)}, u32[]{:S(2)}) collective-permute-start(bf16[9,128,128]{2,1,0:T(8,128)(2,1)S(1)} %collective-permute-done.8.rest_5_.rest_6_), channel_id=1, source_target_pairs={{0,24},{8,0},{16,8},{24,16},{1,25},{9,1},{17,9},{25,17},{2,26},{10... | collective-permute-start | bytes 884744 | tf_op jit(solution)/shard_map/ppermute | solution.py:39

commit v2 on v1

--- a/solution.py
+++ b/solution.py
@@ -100,11 +100,12 @@
             found[jnp.where(hit, at[n], lay.total)] = k
             at[n] = at[n] + hit.astype(jnp.int32)
     total = lay.start[FIRST]
-    for j in range(total):
-        pltpu.make_async_copy(stored_ref.at[found[j]], buf.at[j], sem).start()
-    pltpu.make_async_copy(buf, buf, sem).wait()
+    copies = [pltpu.make_async_copy(stored_ref.at[found[j]], buf.at[j], sem.at[j]) for j in range(total)]
+    for copy in copies:
+        copy.start()
     for s, out in enumerate(outs):
         for j in range(lay.size(s)):
+            copies[lay.start[s] + j].wait()
             out[j] = buf[lay.start[s] + j].T
 
 
@@ -118,7 +119,7 @@
         scratch_shapes=[
             pltpu.VMEM((lay.start[FIRST], block, block), stored.dtype),
             pltpu.SMEM((lay.total + 1,), jnp.int32),
-            pltpu.SemaphoreType.DMA,
+            pltpu.SemaphoreType.DMA((lay.start[FIRST],)),
         ],
         compiler_params=params(FIRST_MIB),
         name="first_stage",

time: 79.8 us -> 79.7 us (level)
  no operation moved by 1% of the time
where the time goes in v2:
time: 79.7 us; the launch traced here: 78.3 us
  waiting for transfers between devices  41.1 us (52%)
  Pallas kernels  23.6 us (30%)
  starting transfers between devices  10.2 us (13%)
  local copies, waits for them, and re-layouts  2.01 us (3%)
  other arithmetic  1.18 us (1%)
    ppermute x12, waiting for transfers between devices, moved(): lax.ppermute(value, axis, [(s, (s + steps) % count) for s in range(count)])  41.1 us
    ppermute x12, starting transfers between devices, moved(): lax.ppermute(value, axis, [(s, (s + steps) % count) for s in range(count)])  10.2 us
    pallas_call x2, Pallas kernels, pick(): pl.pallas_call(functools.partial(pick_kernel, lay, stages, pieces), out_s...  3.5 us
    pallas_call x1, Pallas kernels, next_section(): pl.pallas_call(functools.partial(next_kernel, lay, late), out_shape=jax.S...  3.29 us
    pallas_call x1, Pallas kernels, first_stage(): pl.pallas_call(functools.partial(first_kernel, lay), out_shape=tuple((jax...  3.15 us
    pallas_call x1, Pallas kernels, places(): pl.pallas_call(functools.partial(places_kernel, lay, late), out_shape=(i3...  3 us
    pallas_call x1, Pallas kernels, rest_stages(): pl.pallas_call(functools.partial(rest_kernel, lay), out_shape=shapes + (i...  2.96 us
    pallas_call x1, Pallas kernels, wanted(): pl.pallas_call(functools.partial(wanted_kernel, prods), out_shape=(i32(US...  2.85 us
  transfers between devices with their start and end apart: 12, of which 7 were waited for; matrix products, arithmetic and copies ran while one was open for 2% of the time, Pallas kernels for 22%

profile of v2, /device:TPU:31, one launch (start us, length us, event | category | flops | bytes accessed | tf_op | source)
XLA Modules:
  0.0 78.3 jit_solution(2425592020302407333)
XLA Ops:
  0.0 3.1 %first_stage.1 = bf16[9,128,128]{2,1,0:T(8,128)(2,1)} custom-call(s32[63]{0:T(128)} %bitcast.23, s32[1]{0:T(128)} %bitcast.1.col.token, bf16[63,128,128]{2,1,0:T(8,128)(2,1)} %bitcast.11), custom_call_target="tpu_custom_call" | custom-call | tf_op jit(solution)/shard_map/first_stage/pallas_call | solution.py:114
  3.2 0.1 collective-permute-start.1
  3.3 3.0 %rest_stages.1 = (bf16[10,128,128]{2,1,0:T(8,128)(2,1)S(1)}, bf16[9,128,128]{2,1,0:T(8,128)(2,1)}, bf16[9,128,128]{2,1,0:T(8,128)(2,1)}, bf16[9,128,128]{2,1,0:T...) custom-call(s32[63]{0:T(128)S(1)} %bitcast.24, s32[1]{0:T(128)} %bitcast.1.col.token, ...), custom_call_target="tpu_custom_call" | custom-call | bytes 35000 | tf_op jit(solution)/shard_map/rest_stages/pallas_call | solution.py:163
  6.3 2.1 %collective-permute-start = (bf16[10,128,128]{2,1,0:T(8,128)(2,1)S(1)}, bf16[10,128,128]{2,1,0:T(8,128)(2,1)}, u32[]{:S(2)}, u32[]{:S(2)}) collective-permute-start(bf16[10,128,128]{2,1,0:T(8,128)(2,1)S(1)} %get-tuple-element.63.self_ref), channel_id=1, source_target_pairs={{0,1},{1,2},{2,3},{3,4},{4,5},{5,6},{6,7},{7,0},{8,9},{9,10},{10,1... | collective-permute-start | bytes 983048 | tf_op jit(solution)/shard_map/ppermute | solution.py:39
  8.3 0.7 copy-done.1
  9.1 1.0 %collective-permute-start.2 = (bf16[9,128,128]{2,1,0:T(8,128)(2,1)}, bf16[9,128,128]{2,1,0:T(8,128)(2,1)S(1)}, u32[]{:S(2)}, u32[]{:S(2)}) collective-permute-start(bf16[9,128,128]{2,1,0:T(8,128)(2,1)} %get-tuple-element.68), channel_id=1, source_target_pairs={{0,6},{1,7},{2,0},{3,1},{4,2},{5,3},{6,4},{7,5},{8,14},{9,15},{10,... | collective-permute-start | bytes 884744 | tf_op jit(solution)/shard_map/ppermute | solution.py:39
  10.0 3.1 %collective-permute-start.7 = (bf16[9,128,128]{2,1,0:T(8,128)(2,1)}, bf16[9,128,128]{2,1,0:T(8,128)(2,1)S(1)}, u32[]{:S(2)}, u32[]{:S(2)}) collective-permute-start(bf16[9,128,128]{2,1,0:T(8,128)(2,1)} %get-tuple-element.96), channel_id=1, source_target_pairs={{0,3},{1,4},{2,5},{3,6},{4,7},{5,0},{6,1},{7,2},{8,11},{9,12},{10,... | collective-permute-start | bytes 884744 | tf_op jit(solution)/shard_map/ppermute | solution.py:39
  13.2 0.9 %collective-permute-start.6 = (bf16[9,128,128]{2,1,0:T(8,128)(2,1)}, bf16[9,128,128]{2,1,0:T(8,128)(2,1)}, u32[]{:S(2)}, u32[]{:S(2)}) collective-permute-start(bf16[9,128,128]{2,1,0:T(8,128)(2,1)} %get-tuple-element.95), channel_id=1, source_target_pairs={{0,5},{1,6},{2,7},{3,0},{4,1},{5,2},{6,3},{7,4},{8,13},{9,14},{10,... | collective-permute-start | bytes 884744 | tf_op jit(solution)/shard_map/ppermute | solution.py:39
  14.1 2.1 %collective-permute-done.rest_1_ = bf16[10,128,128]{2,1,0:T(8,128)(2,1)} collective-permute-done((bf16[10,128,128]{2,1,0:T(8,128)(2,1)S(1)}, bf16[10,128,128]{2,1,0:T(8,128)(2,1)}, u32[]{:S(2)}, u32[]{:S(2)}) %collective-permute-start) | collective-permute-done | bytes 327712 | tf_op jit(solution)/shard_map/ppermute | solution.py:39
  16.2 0.3 collective-permute-start.5
  16.5 2.8 %wanted.1 = (s32[24]{0:T(128)}, s32[128]{0:T(128)}, s32[128]{0:T(128)}) custom-call(s32[3,2,128]{2,1,0:T(2,128)} %bitcast.16), custom_call_target="tpu_custom_call" | custom-call | bytes 35000 | tf_op jit(solution)/shard_map/wanted/pallas_call | solution.py:200
  19.3 0.2 collective-permute-done.5.pos_r
  19.5 2.0 %collective-permute-start.4 = (s32[24]{0:T(128)}, s32[24]{0:T(128)S(1)}, u32[]{:S(2)}, u32[]{:S(2)}) collective-permute-start(s32[24]{0:T(128)} %get-tuple-element.76), channel_id=1, source_target_pairs={{0,8},{8,16},{16,24},{24,0},{1,9},{9,17},{17,25},{25,1},{2,10},{10... | collective-permute-start | bytes 296 | tf_op jit(solution)/shard_map/ppermute | solution.py:39
  21.5 1.2 %bitcast_convert_fusion.ids = s32[128]{0:T(128)} fusion(bf16[10,128,128]{2,1,0:T(8,128)(2,1)} %collective-permute-done.rest_1_), kind=kLoop, calls=%fused_computation | loop fusion | flops 128 | bytes 768 | tf_op jit(solution)/shard_map/convert_element_type | solution.py:451
  22.7 0.6 copy-done.14
  23.3 3.0 %places.1 = (s32[3,128]{1,0:T(4,128)}, s32[24]{0:T(128)}) custom-call(s32[3,2,128]{2,1,0:T(2,128)} %bitcast.17, s32[2]{0:T(128)} %bitcast.20, s32[128]{0:T(128)} %get-tuple-element.81.slots_l, s32[128]{0:T(128)} %get-tuple-element.82.slots_r, s32[63]{0:T(128)} %copy-done.8, s32[63]{0:T(128)} %copy-done.13, s32[24]{0:T(128)} %copy-done.14), custom_call_target="tpu_custom_call" | custom-call | tf_op jit(solution)/shard_map/places/pallas_call | solution.py:356
  26.3 2.0 %asked.1.spots = s32[25]{0:T(128)} custom-call(s32[128]{0:T(128)} %bitcast_convert_fusion.ids, s32[63]{0:T(128)} %copy-done.8), custom_call_target="tpu_custom_call" | custom-call | tf_op jit(solution)/shard_map/asked/pallas_call | solution.py:234
  28.3 0.7 collective-permute-done.7.rest_4_.rest_3_
  29.0 15.1 %collective-permute-done.6.rest_5_.rest_4_ = bf16[9,128,128]{2,1,0:T(8,128)(2,1)} collective-permute-done((bf16[9,128,128]{2,1,0:T(8,128)(2,1)}, bf16[9,128,128]{2,1,0:T(8,128)(2,1)}, u32[]{:S(2)}, u32[]{:S(2)}) %collective-permute-start.6) | collective-permute-done | bytes 294944 | tf_op jit(solution)/shard_map/ppermute | solution.py:39
  44.1 0.7 copy-done.10
  44.8 1.8 %pick_right.1 = bf16[24,128,128]{2,1,0:T(8,128)(2,1)S(1)} custom-call(s32[24]{0:T(128)S(1)} %copy-done.10, bf16[63,128,128]{2,1,0:T(8,128)(2,1)S(1)} %bitcast.13, bf16[9,128,128]{2,1,0:T(8,128)(2,1)S(1)} %collective-permute-done.1.rest_0_, bf16[10,128,128]{2,1,0:T(8,128)(2,1)} %collective-permute-done.rest_1_, ...), custom_call_target="tpu_custom_call" | custom-call | tf_op jit(solution)/shard_map/pick_right/pallas_call | solution.py:259
  46.6 0.0 copy-start.4
  46.6 0.0 copy-start.5
  46.6 0.3 collective-permute-start.10
  46.9 13.1 %collective-permute-done.8.rest_5_.rest_6_ = bf16[9,128,128]{2,1,0:T(8,128)(2,1)S(1)} collective-permute-done((bf16[9,128,128]{2,1,0:T(8,128)(2,1)}, bf16[9,128,128]{2,1,0:T(8,128)(2,1)S(1)}, u32[]{:S(2)}, u32[]{:S(2)}) %collective-permute-start.8) | collective-permute-done | bytes 294944 | tf_op jit(solution)/shard_map/ppermute | solution.py:39
  60.0 1.7 %pick_left.1 = bf16[24,128,128]{2,1,0:T(8,128)(2,1)S(1)} custom-call(s32[25]{0:T(128)S(1)} %copy-done.11, bf16[63,128,128]{2,1,0:T(8,128)(2,1)S(1)} %bitcast.14, bf16[9,128,128]{2,1,0:T(8,128)(2,1)S(1)} %collective-permute-done.1.rest_0_, bf16[9,128,128]{2,1,0:T(8,128)(2,1)S(1)} %collective-permute-done.3.rest_2_.rest_1_, ...), custom_call_target="tpu_custom_call" | custom-call | tf_op jit(solution)/shard_map/pick_left/pallas_call | solution.py:259
  61.8 0.3 collective-permute-start.9
  62.0 0.3 collective-permute-start.11
  62.3 2.8 %own_section.1.old = f32[33,128,128]{2,1,0:T(8,128)S(1)} custom-call(s32[3,2,128]{2,1,0:T(2,128)S(1)} %bitcast.19, s32[2]{0:T(128)S(1)} %bitcast.21, s32[63]{0:T(128)S(1)} %copy-done.9, bf16[63,128,128]{2,1,0:T(8,128)(2,1)S(1)} %bitcast.15, bf16[9,128,128]{2,1,0:T(8,128)(2,1)S(1)} %collective-permute-done.1.rest_0_, ...), custom_call_target="tpu_custom_call" | custom-call | bytes 35000 | tf_op jit(solution)/shard_map/own_section/pallas_call | solution.py:320
  65.1 6.9 %collective-permute-done.11.rest_0_ = bf16[9,128,128]{2,1,0:T(8,128)(2,1)S(1)} collective-permute-done((bf16[9,128,128]{2,1,0:T(8,128)(2,1)S(1)}, bf16[9,128,128]{2,1,0:T(8,128)(2,1)S(1)}, u32[]{:S(2)}, u32[]{:S(2)}) %collective-permute-start.11) | collective-permute-done | bytes 294944 | tf_op jit(solution)/shard_map/ppermute | solution.py:39
  72.0 3.0 %collective-permute-done.9.left = bf16[24,128,128]{2,1,0:T(8,128)(2,1)S(1)} collective-permute-done((bf16[24,128,128]{2,1,0:T(8,128)(2,1)S(1)}, bf16[24,128,128]{2,1,0:T(8,128)(2,1)S(1)}, u32[]{:S(2)}, u32[]{:S(2)}) %collective-permute-start.9) | collective-permute-done | bytes 786464 | tf_op jit(solution)/shard_map/ppermute | solution.py:39
  75.0 3.3 %next_section.1 = bf16[32,128,128]{2,1,0:T(8,128)(2,1)} custom-call(s32[1]{0:T(128)} %bitcast.1.col.token, s32[3,128]{1,0:T(4,128)S(1)} %copy-done.6, s32[2]{0:T(128)S(1)} %bitcast.22, f32[33,128,128]{2,1,0:T(8,128)S(1)} %own_section.1.old, bf16[10,128,128]{2,1,0:T(8,128)(2,1)S(1)} %copy-done.2, bf16[24,128,128]{2,1,0:T(8,128)(2,1)S(1)} %collective-permute-done.9.left, ...), custom_call_target="tpu_custom_call" | custom-call | bytes 35000 | tf_op jit(solution)/shard_map/next_section/pallas_call | solution.py:400
  (32 shorter events, 0.1 us)
Async XLA Ops:
  0.0 3.2 %copy-start = (bf16[1,1,63,128,128]{4,3,2,1,0:T(8,128)(2,1)S(1)}, bf16[1,1,63,128,128]{4,3,2,1,0:T(8,128)(2,1)}, u32[]{:S(2)}) copy-start(bf16[1,1,63,128,128]{4,3,2,1,0:T(8,128)(2,1)} %param.4) | copy-start | bytes 6193156
  0.0 3.2 %copy-start.7 = (s32[1,1,63]{2,1,0:T(1,128)S(1)}, s32[1,1,63]{2,1,0:T(1,128)}, u32[]{:S(2)}) copy-start(s32[1,1,63]{2,1,0:T(1,128)} %param.5) | copy-start | bytes 760
  0.0 3.3 %copy-start.3 = (s32[1,1,2,128,3]{3,2,4,1,0:T(2,128)S(1)}, s32[1,1,2,128,3]{3,2,4,1,0:T(2,128)}, u32[]{:S(2)}) copy-start(s32[1,1,2,128,3]{3,2,4,1,0:T(2,128)} %param.6) | copy-start | bytes 9220
  3.2 10.0 %collective-permute-start.1 = (bf16[9,128,128]{2,1,0:T(8,128)(2,1)}, bf16[9,128,128]{2,1,0:T(8,128)(2,1)S(1)}, u32[]{:S(2)}, u32[]{:S(2)}) collective-permute-start(bf16[9,128,128]{2,1,0:T(8,128)(2,1)} %first_stage.1), channel_id=1, source_target_pairs={{0,2},{1,3},{2,4},{3,5},{4,6},{5,7},{6,0},{7,1},{8,10},{9,11},{10,... | collective-permute-start | bytes 884744 | tf_op jit(solution)/shard_map/ppermute | solution.py:39
  6.2 2.1 %copy-start.12 = (bf16[9,128,128]{2,1,0:T(8,128)(2,1)}, bf16[9,128,128]{2,1,0:T(8,128)(2,1)S(1)}, u32[]{:S(2)}) copy-start(bf16[9,128,128]{2,1,0:T(8,128)(2,1)S(1)} %get-tuple-element.100) | copy-start | bytes 884740
  6.2 16.5 %copy-start.8 = (s32[63]{0:T(128)}, s32[63]{0:T(128)S(1)}, u32[]{:S(2)}) copy-start(s32[63]{0:T(128)S(1)} %get-tuple-element.77.pos) | copy-start | bytes 760
  6.3 10.0 %collective-permute-start = (bf16[10,128,128]{2,1,0:T(8,128)(2,1)S(1)}, bf16[10,128,128]{2,1,0:T(8,128)(2,1)}, u32[]{:S(2)}, u32[]{:S(2)}) collective-permute-start(bf16[10,128,128]{2,1,0:T(8,128)(2,1)S(1)} %get-tuple-element.63.self_ref), channel_id=1, source_target_pairs={{0,1},{1,2},{2,3},{3,4},{4,5},{5,6},{6,7},{7,0},{8,9},{9,10},{10,1... | collective-permute-start | bytes 983048 | tf_op jit(solution)/shard_map/ppermute | solution.py:39
  8.3 0.7 copy-start.1
  9.1 17.2 %collective-permute-start.3 = (bf16[9,128,128]{2,1,0:T(8,128)(2,1)}, bf16[9,128,128]{2,1,0:T(8,128)(2,1)S(1)}, u32[]{:S(2)}, u32[]{:S(2)}) collective-permute-start(bf16[9,128,128]{2,1,0:T(8,128)(2,1)} %get-tuple-element.69), channel_id=1, source_target_pairs={{0,7},{1,0},{2,1},{3,2},{4,3},{5,4},{6,5},{7,6},{8,15},{9,8},{10,9... | collective-permute-start | bytes 884744 | tf_op jit(solution)/shard_map/ppermute | solution.py:39
  9.1 17.2 %collective-permute-start.2 = (bf16[9,128,128]{2,1,0:T(8,128)(2,1)}, bf16[9,128,128]{2,1,0:T(8,128)(2,1)S(1)}, u32[]{:S(2)}, u32[]{:S(2)}) collective-permute-start(bf16[9,128,128]{2,1,0:T(8,128)(2,1)} %get-tuple-element.68), channel_id=1, source_target_pairs={{0,6},{1,7},{2,0},{3,1},{4,2},{5,3},{6,4},{7,5},{8,14},{9,15},{10,... | collective-permute-start | bytes 884744 | tf_op jit(solution)/shard_map/ppermute | solution.py:39
  10.0 19.0 %collective-permute-start.7 = (bf16[9,128,128]{2,1,0:T(8,128)(2,1)}, bf16[9,128,128]{2,1,0:T(8,128)(2,1)S(1)}, u32[]{:S(2)}, u32[]{:S(2)}) collective-permute-start(bf16[9,128,128]{2,1,0:T(8,128)(2,1)} %get-tuple-element.96), channel_id=1, source_target_pairs={{0,3},{1,4},{2,5},{3,6},{4,7},{5,0},{6,1},{7,2},{8,11},{9,12},{10,... | collective-permute-start | bytes 884744 | tf_op jit(solution)/shard_map/ppermute | solution.py:39
  13.2 30.9 %collective-permute-start.6 = (bf16[9,128,128]{2,1,0:T(8,128)(2,1)}, bf16[9,128,128]{2,1,0:T(8,128)(2,1)}, u32[]{:S(2)}, u32[]{:S(2)}) collective-permute-start(bf16[9,128,128]{2,1,0:T(8,128)(2,1)} %get-tuple-element.95), channel_id=1, source_target_pairs={{0,5},{1,6},{2,7},{3,0},{4,1},{5,2},{6,3},{7,4},{8,13},{9,14},{10,... | collective-permute-start | bytes 884744 | tf_op jit(solution)/shard_map/ppermute | solution.py:39
  16.2 3.3 %collective-permute-start.5 = (s32[63]{0:T(128)S(1)}, s32[63]{0:T(128)S(1)}, u32[]{:S(2)}, u32[]{:S(2)}) collective-permute-start(s32[63]{0:T(128)S(1)} %get-tuple-element.77.pos), channel_id=1, source_target_pairs={{0,24},{8,0},{16,8},{24,16},{1,25},{9,1},{17,9},{25,17},{2,26},{10... | collective-permute-start | bytes 764 | tf_op jit(solution)/shard_map/ppermute | solution.py:39
  19.5 3.2 %copy-start.13 = (s32[63]{0:T(128)}, s32[63]{0:T(128)S(1)}, u32[]{:S(2)}) copy-start(s32[63]{0:T(128)S(1)} %collective-permute-done.5.pos_r) | copy-start | bytes 760
  19.5 3.2 %collective-permute-start.4 = (s32[24]{0:T(128)}, s32[24]{0:T(128)S(1)}, u32[]{:S(2)}, u32[]{:S(2)}) collective-permute-start(s32[24]{0:T(128)} %get-tuple-element.76), channel_id=1, source_target_pairs={{0,8},{8,16},{16,24},{24,0},{1,9},{9,17},{17,25},{25,1},{2,10},{10... | collective-permute-start | bytes 296 | tf_op jit(solution)/shard_map/ppermute | solution.py:39
  22.7 0.6 copy-start.14
  44.1 15.9 %collective-permute-start.8 = (bf16[9,128,128]{2,1,0:T(8,128)(2,1)}, bf16[9,128,128]{2,1,0:T(8,128)(2,1)S(1)}, u32[]{:S(2)}, u32[]{:S(2)}) collective-permute-start(bf16[9,128,128]{2,1,0:T(8,128)(2,1)} %copy-done.12), channel_id=1, source_target_pairs={{0,4},{1,5},{2,6},{3,7},{4,0},{5,1},{6,2},{7,3},{8,12},{9,13},{10,... | collective-permute-start | bytes 884744 | tf_op jit(solution)/shard_map/ppermute | solution.py:39
  44.1 0.7 copy-start.10
  44.8 15.3 %copy-start.11 = (s32[25]{0:T(128)S(1)}, s32[25]{0:T(128)}, u32[]{:S(2)}) copy-start(s32[25]{0:T(128)} %asked.1.spots) | copy-start | bytes 304
  46.6 15.7 %copy-start.4 = (s32[1,1,2,128,3]{3,2,4,1,0:T(2,128)S(1)}, s32[1,1,2,128,3]{3,2,4,1,0:T(2,128)}, u32[]{:S(2)}) copy-start(s32[1,1,2,128,3]{3,2,4,1,0:T(2,128)} %param.6) | copy-start | bytes 9220
  46.6 15.7 %copy-start.5 = (s32[1,1,2]{2,1,0:T(1,128)S(1)}, s32[1,1,2]{2,1,0:T(1,128)}, u32[]{:S(2)}) copy-start(s32[1,1,2]{2,1,0:T(1,128)} %param.7) | copy-start | bytes 28
  46.6 15.7 %copy-start.9 = (s32[63]{0:T(128)S(1)}, s32[63]{0:T(128)}, u32[]{:S(2)}) copy-start(s32[63]{0:T(128)} %copy-done.8) | copy-start | bytes 760
  46.6 25.4 %collective-permute-start.10 = (bf16[24,128,128]{2,1,0:T(8,128)(2,1)S(1)}, bf16[24,128,128]{2,1,0:T(8,128)(2,1)S(1)}, u32[]{:S(2)}, u32[]{:S(2)}) collective-permute-start(bf16[24,128,128]{2,1,0:T(8,128)(2,1)S(1)} %pick_right.1), channel_id=1, source_target_pairs={{0,24},{8,0},{16,8},{24,16},{1,25},{9,1},{17,9},{25,17},{2,26},{10... | collective-permute-start | bytes 2359304 | tf_op jit(solution)/shard_map/ppermute | solution.py:39
  61.8 13.3 %copy-start.2 = (bf16[10,128,128]{2,1,0:T(8,128)(2,1)S(1)}, bf16[10,128,128]{2,1,0:T(8,128)(2,1)}, u32[]{:S(2)}) copy-start(bf16[10,128,128]{2,1,0:T(8,128)(2,1)} %copy-done.1) | copy-start | bytes 983044
  61.8 13.3 %copy-start.6 = (s32[3,128]{1,0:T(4,128)S(1)}, s32[3,128]{1,0:T(4,128)}, u32[]{:S(2)}) copy-start(s32[3,128]{1,0:T(4,128)} %get-tuple-element.114.spots) | copy-start | bytes 4612
  61.8 13.3 %collective-permute-start.9 = (bf16[24,128,128]{2,1,0:T(8,128)(2,1)S(1)}, bf16[24,128,128]{2,1,0:T(8,128)(2,1)S(1)}, u32[]{:S(2)}, u32[]{:S(2)}) collective-permute-start(bf16[24,128,128]{2,1,0:T(8,128)(2,1)S(1)} %pick_left.1), channel_id=1, source_target_pairs={{0,7},{1,0},{2,1},{3,2},{4,3},{5,4},{6,5},{7,6},{8,15},{9,8},{10,9... | collective-permute-start | bytes 2359304 | tf_op jit(solution)/shard_map/ppermute | solution.py:39
  62.0 10.0 %collective-permute-start.11 = (bf16[9,128,128]{2,1,0:T(8,128)(2,1)S(1)}, bf16[9,128,128]{2,1,0:T(8,128)(2,1)S(1)}, u32[]{:S(2)}, u32[]{:S(2)}) collective-permute-start(bf16[9,128,128]{2,1,0:T(8,128)(2,1)S(1)} %collective-permute-done.8.rest_5_.rest_6_), channel_id=1, source_target_pairs={{0,24},{8,0},{16,8},{24,16},{1,25},{9,1},{17,9},{25,17},{2,26},{10... | collective-permute-start | bytes 884744 | tf_op jit(solution)/shard_map/ppermute | solution.py:39

commit v3 on v1

--- a/solution.py
+++ b/solution.py
@@ -92,20 +92,29 @@
     for n, offset in enumerate(d for stage in lay.stages[:FIRST] for d in stage):
         goal = col[0] + offset
         goals.append(jnp.where(goal >= lay.cols, goal - lay.cols, goal))
-    at = [jnp.int32(n * lay.cap) for n in range(len(goals))]
-    for k in range(lay.stored):
-        target = tgt[k]
-        for n, goal in enumerate(goals):
-            hit = target == goal
+
+    def find(k, at):
+        hits = [tgt[k] == goal for goal in goals]
+        for n, hit in enumerate(hits):
             found[jnp.where(hit, at[n], lay.total)] = k
-            at[n] = at[n] + hit.astype(jnp.int32)
-    total = lay.start[FIRST]
-    for j in range(total):
+        return tuple(n + hit.astype(jnp.int32) for n, hit in zip(at, hits))
+
+    starts = tuple(jnp.int32(n * lay.cap) for n in range(len(goals)))
+    lax.fori_loop(0, lay.stored, find, starts, unroll=9 if lay.stored % 9 == 0 else 1)
+
+    def fetch(j, carry):
         pltpu.make_async_copy(stored_ref.at[found[j]], buf.at[j], sem).start()
+        return carry
+
+    lax.fori_loop(0, lay.start[FIRST], fetch, 0)
     pltpu.make_async_copy(buf, buf, sem).wait()
     for s, out in enumerate(outs):
-        for j in range(lay.size(s)):
+
+        def flip(j, carry, s=s, out=out):
             out[j] = buf[lay.start[s] + j].T
+            return carry
+
+        lax.fori_loop(0, lay.size(s), flip, 0, unroll=3 if lay.size(s) % 3 == 0 else 1)
 
 
 def first_stage(lay, targets, col, stored):

time: 79.8 us -> 80.1 us (level)
  the two profiles are of different devices: /device:TPU:31 before, /device:TPU:1 now
where the time goes in v3:
time: 80.1 us; the launch traced here: 78.5 us
  waiting for transfers between devices  34.6 us (43%)
  Pallas kernels  23.6 us (29%)
  starting transfers between devices  17 us (21%)
  local copies, waits for them, and re-layouts  2.02 us (3%)
  other arithmetic  1.19 us (1%)
    ppermute x12, waiting for transfers between devices, moved(): lax.ppermute(value, axis, [(s, (s + steps) % count) for s in range(count)])  34.6 us
    ppermute x12, starting transfers between devices, moved(): lax.ppermute(value, axis, [(s, (s + steps) % count) for s in range(count)])  17 us
    pallas_call x2, Pallas kernels, pick(): pl.pallas_call(functools.partial(pick_kernel, lay, stages, pieces), out_s...  3.5 us
    pallas_call x1, Pallas kernels, next_section(): pl.pallas_call(functools.partial(next_kernel, lay, late), out_shape=jax.S...  3.29 us
    pallas_call x1, Pallas kernels, own_section(): pl.pallas_call(functools.partial(own_kernel, lay, prods), out_shape=jax.S...  3.17 us
    pallas_call x1, Pallas kernels, places(): pl.pallas_call(functools.partial(places_kernel, lay, late), out_shape=(i3...  3 us
    pallas_call x1, Pallas kernels, rest_stages(): pl.pallas_call(functools.partial(rest_kernel, lay), out_shape=shapes + (i...  2.95 us
    pallas_call x1, Pallas kernels, first_stage(): pl.pallas_call(functools.partial(first_kernel, lay), out_shape=tuple((jax...  2.85 us
  transfers between devices with their start and end apart: 12, of which 6 were waited for; matrix products, arithmetic and copies ran while one was open for 2% of the time, Pallas kernels for 22%

profile of v3, /device:TPU:1, one launch (start us, length us, event | category | flops | bytes accessed | tf_op | source)
XLA Modules:
  0.0 78.5 jit_solution(4680730840761958472)
XLA Ops:
  0.0 2.8 %first_stage.1 = bf16[9,128,128]{2,1,0:T(8,128)(2,1)} custom-call(s32[63]{0:T(128)} %bitcast.23, s32[1]{0:T(128)} %bitcast.1.col.token, bf16[63,128,128]{2,1,0:T(8,128)(2,1)} %bitcast.11), custom_call_target="tpu_custom_call" | custom-call | tf_op jit(solution)/shard_map/first_stage/pallas_call | solution.py:122
  2.9 2.2 %collective-permute-start.1 = (bf16[9,128,128]{2,1,0:T(8,128)(2,1)}, bf16[9,128,128]{2,1,0:T(8,128)(2,1)S(1)}, u32[]{:S(2)}, u32[]{:S(2)}) collective-permute-start(bf16[9,128,128]{2,1,0:T(8,128)(2,1)} %first_stage.1), channel_id=1, source_target_pairs={{0,2},{1,3},{2,4},{3,5},{4,6},{5,7},{6,0},{7,1},{8,10},{9,11},{10,... | collective-permute-start | bytes 884744 | tf_op jit(solution)/shard_map/ppermute | solution.py:39
  5.1 3.0 %rest_stages.1 = (bf16[10,128,128]{2,1,0:T(8,128)(2,1)S(1)}, bf16[9,128,128]{2,1,0:T(8,128)(2,1)}, bf16[9,128,128]{2,1,0:T(8,128)(2,1)}, bf16[9,128,128]{2,1,0:T...) custom-call(s32[63]{0:T(128)S(1)} %bitcast.24, s32[1]{0:T(128)} %bitcast.1.col.token, ...), custom_call_target="tpu_custom_call" | custom-call | bytes 35000 | tf_op jit(solution)/shard_map/rest_stages/pallas_call | solution.py:171
  8.0 2.2 %collective-permute-start = (bf16[10,128,128]{2,1,0:T(8,128)(2,1)S(1)}, bf16[10,128,128]{2,1,0:T(8,128)(2,1)}, u32[]{:S(2)}, u32[]{:S(2)}) collective-permute-start(bf16[10,128,128]{2,1,0:T(8,128)(2,1)S(1)} %get-tuple-element.63.self_ref), channel_id=1, source_target_pairs={{0,1},{1,2},{2,3},{3,4},{4,5},{5,6},{6,7},{7,0},{8,9},{9,10},{10,1... | collective-permute-start | bytes 983048 | tf_op jit(solution)/shard_map/ppermute | solution.py:39
  10.2 0.7 copy-done.1
  11.0 2.0 %collective-permute-start.2 = (bf16[9,128,128]{2,1,0:T(8,128)(2,1)}, bf16[9,128,128]{2,1,0:T(8,128)(2,1)S(1)}, u32[]{:S(2)}, u32[]{:S(2)}) collective-permute-start(bf16[9,128,128]{2,1,0:T(8,128)(2,1)} %get-tuple-element.68), channel_id=1, source_target_pairs={{0,6},{1,7},{2,0},{3,1},{4,2},{5,3},{6,4},{7,5},{8,14},{9,15},{10,... | collective-permute-start | bytes 884744 | tf_op jit(solution)/shard_map/ppermute | solution.py:39
  13.0 1.2 %collective-permute-start.7 = (bf16[9,128,128]{2,1,0:T(8,128)(2,1)}, bf16[9,128,128]{2,1,0:T(8,128)(2,1)S(1)}, u32[]{:S(2)}, u32[]{:S(2)}) collective-permute-start(bf16[9,128,128]{2,1,0:T(8,128)(2,1)} %get-tuple-element.96), channel_id=1, source_target_pairs={{0,3},{1,4},{2,5},{3,6},{4,7},{5,0},{6,1},{7,2},{8,11},{9,12},{10,... | collective-permute-start | bytes 884744 | tf_op jit(solution)/shard_map/ppermute | solution.py:39
  14.2 3.6 %collective-permute-start.6 = (bf16[9,128,128]{2,1,0:T(8,128)(2,1)}, bf16[9,128,128]{2,1,0:T(8,128)(2,1)}, u32[]{:S(2)}, u32[]{:S(2)}) collective-permute-start(bf16[9,128,128]{2,1,0:T(8,128)(2,1)} %get-tuple-element.95), channel_id=1, source_target_pairs={{0,5},{1,6},{2,7},{3,0},{4,1},{5,2},{6,3},{7,4},{8,13},{9,14},{10,... | collective-permute-start | bytes 884744 | tf_op jit(solution)/shard_map/ppermute | solution.py:39
  17.7 2.2 %collective-permute-start.5 = (s32[63]{0:T(128)S(1)}, s32[63]{0:T(128)S(1)}, u32[]{:S(2)}, u32[]{:S(2)}) collective-permute-start(s32[63]{0:T(128)S(1)} %get-tuple-element.77.pos), channel_id=1, source_target_pairs={{0,24},{8,0},{16,8},{24,16},{1,25},{9,1},{17,9},{25,17},{2,26},{10... | collective-permute-start | bytes 764 | tf_op jit(solution)/shard_map/ppermute | solution.py:39
  19.9 2.8 %wanted.1 = (s32[24]{0:T(128)}, s32[128]{0:T(128)}, s32[128]{0:T(128)}) custom-call(s32[3,2,128]{2,1,0:T(2,128)} %bitcast.16), custom_call_target="tpu_custom_call" | custom-call | bytes 35000 | tf_op jit(solution)/shard_map/wanted/pallas_call | solution.py:208
  22.8 0.1 collective-permute-start.4
  22.9 1.2 %bitcast_convert_fusion.ids = s32[128]{0:T(128)} fusion(bf16[10,128,128]{2,1,0:T(8,128)(2,1)} %collective-permute-done.rest_1_), kind=kLoop, calls=%fused_computation | loop fusion | flops 128 | bytes 768 | tf_op jit(solution)/shard_map/convert_element_type | solution.py:459
  24.0 2.4 %collective-permute-done.4.asked_r = s32[24]{0:T(128)S(1)} collective-permute-done((s32[24]{0:T(128)}, s32[24]{0:T(128)S(1)}, u32[]{:S(2)}, u32[]{:S(2)}) %collective-permute-start.4) | collective-permute-done | bytes 128 | tf_op jit(solution)/shard_map/ppermute | solution.py:39
  26.5 0.6 copy-done.14
  27.1 3.0 %places.1 = (s32[3,128]{1,0:T(4,128)}, s32[24]{0:T(128)}) custom-call(s32[3,2,128]{2,1,0:T(2,128)} %bitcast.17, s32[2]{0:T(128)} %bitcast.20, s32[128]{0:T(128)} %get-tuple-element.81.slots_l, s32[128]{0:T(128)} %get-tuple-element.82.slots_r, s32[63]{0:T(128)} %copy-done.8, s32[63]{0:T(128)} %copy-done.13, s32[24]{0:T(128)} %copy-done.14), custom_call_target="tpu_custom_call" | custom-call | tf_op jit(solution)/shard_map/places/pallas_call | solution.py:364
  30.1 2.0 %asked.1.spots = s32[25]{0:T(128)} custom-call(s32[128]{0:T(128)} %bitcast_convert_fusion.ids, s32[63]{0:T(128)} %copy-done.8), custom_call_target="tpu_custom_call" | custom-call | tf_op jit(solution)/shard_map/asked/pallas_call | solution.py:242
  32.1 2.3 %collective-permute-done.7.rest_4_.rest_3_ = bf16[9,128,128]{2,1,0:T(8,128)(2,1)S(1)} collective-permute-done((bf16[9,128,128]{2,1,0:T(8,128)(2,1)}, bf16[9,128,128]{2,1,0:T(8,128)(2,1)S(1)}, u32[]{:S(2)}, u32[]{:S(2)}) %collective-permute-start.7) | collective-permute-done | bytes 294944 | tf_op jit(solution)/shard_map/ppermute | solution.py:39
  34.4 12.2 %collective-permute-done.6.rest_5_.rest_4_ = bf16[9,128,128]{2,1,0:T(8,128)(2,1)} collective-permute-done((bf16[9,128,128]{2,1,0:T(8,128)(2,1)}, bf16[9,128,128]{2,1,0:T(8,128)(2,1)}, u32[]{:S(2)}, u32[]{:S(2)}) %collective-permute-start.6) | collective-permute-done | bytes 294944 | tf_op jit(solution)/shard_map/ppermute | solution.py:39
  46.6 0.7 copy-done.10
  47.3 1.8 %pick_right.1 = bf16[24,128,128]{2,1,0:T(8,128)(2,1)S(1)} custom-call(s32[24]{0:T(128)S(1)} %copy-done.10, bf16[63,128,128]{2,1,0:T(8,128)(2,1)S(1)} %bitcast.13, bf16[9,128,128]{2,1,0:T(8,128)(2,1)S(1)} %collective-permute-done.1.rest_0_, bf16[10,128,128]{2,1,0:T(8,128)(2,1)} %collective-permute-done.rest_1_, ...), custom_call_target="tpu_custom_call" | custom-call | tf_op jit(solution)/shard_map/pick_right/pallas_call | solution.py:267
  49.1 0.0 copy-start.4
  49.1 0.0 copy-start.5
  49.1 2.2 %collective-permute-start.10 = (bf16[24,128,128]{2,1,0:T(8,128)(2,1)S(1)}, bf16[24,128,128]{2,1,0:T(8,128)(2,1)S(1)}, u32[]{:S(2)}, u32[]{:S(2)}) collective-permute-start(bf16[24,128,128]{2,1,0:T(8,128)(2,1)S(1)} %pick_right.1), channel_id=1, source_target_pairs={{0,24},{8,0},{16,8},{24,16},{1,25},{9,1},{17,9},{25,17},{2,26},{10... | collective-permute-start | bytes 2359304 | tf_op jit(solution)/shard_map/ppermute | solution.py:39
  51.4 10.7 %collective-permute-done.8.rest_5_.rest_6_ = bf16[9,128,128]{2,1,0:T(8,128)(2,1)S(1)} collective-permute-done((bf16[9,128,128]{2,1,0:T(8,128)(2,1)}, bf16[9,128,128]{2,1,0:T(8,128)(2,1)S(1)}, u32[]{:S(2)}, u32[]{:S(2)}) %collective-permute-start.8) | collective-permute-done | bytes 294944 | tf_op jit(solution)/shard_map/ppermute | solution.py:39
  62.0 1.7 %pick_left.1 = bf16[24,128,128]{2,1,0:T(8,128)(2,1)S(1)} custom-call(s32[25]{0:T(128)S(1)} %copy-done.11, bf16[63,128,128]{2,1,0:T(8,128)(2,1)S(1)} %bitcast.14, bf16[9,128,128]{2,1,0:T(8,128)(2,1)S(1)} %collective-permute-done.1.rest_0_, bf16[9,128,128]{2,1,0:T(8,128)(2,1)S(1)} %collective-permute-done.3.rest_2_.rest_1_, ...), custom_call_target="tpu_custom_call" | custom-call | tf_op jit(solution)/shard_map/pick_left/pallas_call | solution.py:267
  63.8 0.0 copy-start.2
  63.8 0.4 collective-permute-start.9
  64.2 0.9 %collective-permute-start.11 = (bf16[9,128,128]{2,1,0:T(8,128)(2,1)S(1)}, bf16[9,128,128]{2,1,0:T(8,128)(2,1)S(1)}, u32[]{:S(2)}, u32[]{:S(2)}) collective-permute-start(bf16[9,128,128]{2,1,0:T(8,128)(2,1)S(1)} %collective-permute-done.8.rest_5_.rest_6_), channel_id=1, source_target_pairs={{0,24},{8,0},{16,8},{24,16},{1,25},{9,1},{17,9},{25,17},{2,26},{10... | collective-permute-start | bytes 884744 | tf_op jit(solution)/shard_map/ppermute | solution.py:39
  65.1 3.2 %own_section.1.old = f32[33,128,128]{2,1,0:T(8,128)S(1)} custom-call(s32[3,2,128]{2,1,0:T(2,128)S(1)} %bitcast.19, s32[2]{0:T(128)S(1)} %bitcast.21, s32[63]{0:T(128)S(1)} %copy-done.9, bf16[63,128,128]{2,1,0:T(8,128)(2,1)S(1)} %bitcast.15, bf16[9,128,128]{2,1,0:T(8,128)(2,1)S(1)} %collective-permute-done.1.rest_0_, ...), custom_call_target="tpu_custom_call" | custom-call | bytes 35000 | tf_op jit(solution)/shard_map/own_section/pallas_call | solution.py:328
  68.3 5.8 %collective-permute-done.11.rest_0_ = bf16[9,128,128]{2,1,0:T(8,128)(2,1)S(1)} collective-permute-done((bf16[9,128,128]{2,1,0:T(8,128)(2,1)S(1)}, bf16[9,128,128]{2,1,0:T(8,128)(2,1)S(1)}, u32[]{:S(2)}, u32[]{:S(2)}) %collective-permute-start.11) | collective-permute-done | bytes 294944 | tf_op jit(solution)/shard_map/ppermute | solution.py:39
  74.1 1.2 %collective-permute-done.9.left = bf16[24,128,128]{2,1,0:T(8,128)(2,1)S(1)} collective-permute-done((bf16[24,128,128]{2,1,0:T(8,128)(2,1)S(1)}, bf16[24,128,128]{2,1,0:T(8,128)(2,1)S(1)}, u32[]{:S(2)}, u32[]{:S(2)}) %collective-permute-start.9) | collective-permute-done | bytes 786464 | tf_op jit(solution)/shard_map/ppermute | solution.py:39
  75.2 3.3 %next_section.1 = bf16[32,128,128]{2,1,0:T(8,128)(2,1)} custom-call(s32[1]{0:T(128)} %bitcast.1.col.token, s32[3,128]{1,0:T(4,128)S(1)} %copy-done.6, s32[2]{0:T(128)S(1)} %bitcast.22, f32[33,128,128]{2,1,0:T(8,128)S(1)} %own_section.1.old, bf16[10,128,128]{2,1,0:T(8,128)(2,1)S(1)} %copy-done.2, bf16[24,128,128]{2,1,0:T(8,128)(2,1)S(1)} %collective-permute-done.9.left, ...), custom_call_target="tpu_custom_call" | custom-call | bytes 35000 | tf_op jit(solution)/shard_map/next_section/pallas_call | solution.py:408
  (32 shorter events, 0.1 us)
Async XLA Ops:
  0.0 5.1 %copy-start = (bf16[1,1,63,128,128]{4,3,2,1,0:T(8,128)(2,1)S(1)}, bf16[1,1,63,128,128]{4,3,2,1,0:T(8,128)(2,1)}, u32[]{:S(2)}) copy-start(bf16[1,1,63,128,128]{4,3,2,1,0:T(8,128)(2,1)} %param.4) | copy-start | bytes 6193156
  0.0 5.1 %copy-start.7 = (s32[1,1,63]{2,1,0:T(1,128)S(1)}, s32[1,1,63]{2,1,0:T(1,128)}, u32[]{:S(2)}) copy-start(s32[1,1,63]{2,1,0:T(1,128)} %param.5) | copy-start | bytes 760
  0.0 5.1 %copy-start.3 = (s32[1,1,2,128,3]{3,2,4,1,0:T(2,128)S(1)}, s32[1,1,2,128,3]{3,2,4,1,0:T(2,128)}, u32[]{:S(2)}) copy-start(s32[1,1,2,128,3]{3,2,4,1,0:T(2,128)} %param.6) | copy-start | bytes 9220
  2.9 11.3 %collective-permute-start.1 = (bf16[9,128,128]{2,1,0:T(8,128)(2,1)}, bf16[9,128,128]{2,1,0:T(8,128)(2,1)S(1)}, u32[]{:S(2)}, u32[]{:S(2)}) collective-permute-start(bf16[9,128,128]{2,1,0:T(8,128)(2,1)} %first_stage.1), channel_id=1, source_target_pairs={{0,2},{1,3},{2,4},{3,5},{4,6},{5,7},{6,0},{7,1},{8,10},{9,11},{10,... | collective-permute-start | bytes 884744 | tf_op jit(solution)/shard_map/ppermute | solution.py:39
  8.0 2.2 %copy-start.12 = (bf16[9,128,128]{2,1,0:T(8,128)(2,1)}, bf16[9,128,128]{2,1,0:T(8,128)(2,1)S(1)}, u32[]{:S(2)}) copy-start(bf16[9,128,128]{2,1,0:T(8,128)(2,1)S(1)} %get-tuple-element.100) | copy-start | bytes 884740
  8.0 18.5 %copy-start.8 = (s32[63]{0:T(128)}, s32[63]{0:T(128)S(1)}, u32[]{:S(2)}) copy-start(s32[63]{0:T(128)S(1)} %get-tuple-element.77.pos) | copy-start | bytes 760
  8.0 9.7 %collective-permute-start = (bf16[10,128,128]{2,1,0:T(8,128)(2,1)S(1)}, bf16[10,128,128]{2,1,0:T(8,128)(2,1)}, u32[]{:S(2)}, u32[]{:S(2)}) collective-permute-start(bf16[10,128,128]{2,1,0:T(8,128)(2,1)S(1)} %get-tuple-element.63.self_ref), channel_id=1, source_target_pairs={{0,1},{1,2},{2,3},{3,4},{4,5},{5,6},{6,7},{7,0},{8,9},{9,10},{10,1... | collective-permute-start | bytes 983048 | tf_op jit(solution)/shard_map/ppermute | solution.py:39
  10.2 0.7 copy-start.1
  11.0 19.1 %collective-permute-start.3 = (bf16[9,128,128]{2,1,0:T(8,128)(2,1)}, bf16[9,128,128]{2,1,0:T(8,128)(2,1)S(1)}, u32[]{:S(2)}, u32[]{:S(2)}) collective-permute-start(bf16[9,128,128]{2,1,0:T(8,128)(2,1)} %get-tuple-element.69), channel_id=1, source_target_pairs={{0,7},{1,0},{2,1},{3,2},{4,3},{5,4},{6,5},{7,6},{8,15},{9,8},{10,9... | collective-permute-start | bytes 884744 | tf_op jit(solution)/shard_map/ppermute | solution.py:39
  11.0 19.1 %collective-permute-start.2 = (bf16[9,128,128]{2,1,0:T(8,128)(2,1)}, bf16[9,128,128]{2,1,0:T(8,128)(2,1)S(1)}, u32[]{:S(2)}, u32[]{:S(2)}) collective-permute-start(bf16[9,128,128]{2,1,0:T(8,128)(2,1)} %get-tuple-element.68), channel_id=1, source_target_pairs={{0,6},{1,7},{2,0},{3,1},{4,2},{5,3},{6,4},{7,5},{8,14},{9,15},{10,... | collective-permute-start | bytes 884744 | tf_op jit(solution)/shard_map/ppermute | solution.py:39
  13.0 21.4 %collective-permute-start.7 = (bf16[9,128,128]{2,1,0:T(8,128)(2,1)}, bf16[9,128,128]{2,1,0:T(8,128)(2,1)S(1)}, u32[]{:S(2)}, u32[]{:S(2)}) collective-permute-start(bf16[9,128,128]{2,1,0:T(8,128)(2,1)} %get-tuple-element.96), channel_id=1, source_target_pairs={{0,3},{1,4},{2,5},{3,6},{4,7},{5,0},{6,1},{7,2},{8,11},{9,12},{10,... | collective-permute-start | bytes 884744 | tf_op jit(solution)/shard_map/ppermute | solution.py:39
  14.2 32.4 %collective-permute-start.6 = (bf16[9,128,128]{2,1,0:T(8,128)(2,1)}, bf16[9,128,128]{2,1,0:T(8,128)(2,1)}, u32[]{:S(2)}, u32[]{:S(2)}) collective-permute-start(bf16[9,128,128]{2,1,0:T(8,128)(2,1)} %get-tuple-element.95), channel_id=1, source_target_pairs={{0,5},{1,6},{2,7},{3,0},{4,1},{5,2},{6,3},{7,4},{8,13},{9,14},{10,... | collective-permute-start | bytes 884744 | tf_op jit(solution)/shard_map/ppermute | solution.py:39
  17.7 5.0 %collective-permute-start.5 = (s32[63]{0:T(128)S(1)}, s32[63]{0:T(128)S(1)}, u32[]{:S(2)}, u32[]{:S(2)}) collective-permute-start(s32[63]{0:T(128)S(1)} %get-tuple-element.77.pos), channel_id=1, source_target_pairs={{0,24},{8,0},{16,8},{24,16},{1,25},{9,1},{17,9},{25,17},{2,26},{10... | collective-permute-start | bytes 764 | tf_op jit(solution)/shard_map/ppermute | solution.py:39
  22.8 3.7 %copy-start.13 = (s32[63]{0:T(128)}, s32[63]{0:T(128)S(1)}, u32[]{:S(2)}) copy-start(s32[63]{0:T(128)S(1)} %collective-permute-done.5.pos_r) | copy-start | bytes 760
  22.8 3.7 %collective-permute-start.4 = (s32[24]{0:T(128)}, s32[24]{0:T(128)S(1)}, u32[]{:S(2)}, u32[]{:S(2)}) collective-permute-start(s32[24]{0:T(128)} %get-tuple-element.76), channel_id=1, source_target_pairs={{0,8},{8,16},{16,24},{24,0},{1,9},{9,17},{17,25},{25,1},{2,10},{10... | collective-permute-start | bytes 296 | tf_op jit(solution)/shard_map/ppermute | solution.py:39
  26.5 0.6 copy-start.14
  46.6 15.4 %collective-permute-start.8 = (bf16[9,128,128]{2,1,0:T(8,128)(2,1)}, bf16[9,128,128]{2,1,0:T(8,128)(2,1)S(1)}, u32[]{:S(2)}, u32[]{:S(2)}) collective-permute-start(bf16[9,128,128]{2,1,0:T(8,128)(2,1)} %copy-done.12), channel_id=1, source_target_pairs={{0,4},{1,5},{2,6},{3,7},{4,0},{5,1},{6,2},{7,3},{8,12},{9,13},{10,... | collective-permute-start | bytes 884744 | tf_op jit(solution)/shard_map/ppermute | solution.py:39
  46.6 0.7 copy-start.10
  47.3 14.8 %copy-start.11 = (s32[25]{0:T(128)S(1)}, s32[25]{0:T(128)}, u32[]{:S(2)}) copy-start(s32[25]{0:T(128)} %asked.1.spots) | copy-start | bytes 304
  49.1 16.0 %copy-start.4 = (s32[1,1,2,128,3]{3,2,4,1,0:T(2,128)S(1)}, s32[1,1,2,128,3]{3,2,4,1,0:T(2,128)}, u32[]{:S(2)}) copy-start(s32[1,1,2,128,3]{3,2,4,1,0:T(2,128)} %param.6) | copy-start | bytes 9220
  49.1 16.0 %copy-start.5 = (s32[1,1,2]{2,1,0:T(1,128)S(1)}, s32[1,1,2]{2,1,0:T(1,128)}, u32[]{:S(2)}) copy-start(s32[1,1,2]{2,1,0:T(1,128)} %param.7) | copy-start | bytes 28
  49.1 16.0 %copy-start.9 = (s32[63]{0:T(128)S(1)}, s32[63]{0:T(128)}, u32[]{:S(2)}) copy-start(s32[63]{0:T(128)} %copy-done.8) | copy-start | bytes 760
  49.1 24.9 %collective-permute-start.10 = (bf16[24,128,128]{2,1,0:T(8,128)(2,1)S(1)}, bf16[24,128,128]{2,1,0:T(8,128)(2,1)S(1)}, u32[]{:S(2)}, u32[]{:S(2)}) collective-permute-start(bf16[24,128,128]{2,1,0:T(8,128)(2,1)S(1)} %pick_right.1), channel_id=1, source_target_pairs={{0,24},{8,0},{16,8},{24,16},{1,25},{9,1},{17,9},{25,17},{2,26},{10... | collective-permute-start | bytes 2359304 | tf_op jit(solution)/shard_map/ppermute | solution.py:39
  63.8 11.5 %copy-start.2 = (bf16[10,128,128]{2,1,0:T(8,128)(2,1)S(1)}, bf16[10,128,128]{2,1,0:T(8,128)(2,1)}, u32[]{:S(2)}) copy-start(bf16[10,128,128]{2,1,0:T(8,128)(2,1)} %copy-done.1) | copy-start | bytes 983044
  63.8 11.5 %copy-start.6 = (s32[3,128]{1,0:T(4,128)S(1)}, s32[3,128]{1,0:T(4,128)}, u32[]{:S(2)}) copy-start(s32[3,128]{1,0:T(4,128)} %get-tuple-element.114.spots) | copy-start | bytes 4612
  63.8 11.5 %collective-permute-start.9 = (bf16[24,128,128]{2,1,0:T(8,128)(2,1)S(1)}, bf16[24,128,128]{2,1,0:T(8,128)(2,1)S(1)}, u32[]{:S(2)}, u32[]{:S(2)}) collective-permute-start(bf16[24,128,128]{2,1,0:T(8,128)(2,1)S(1)} %pick_left.1), channel_id=1, source_target_pairs={{0,7},{1,0},{2,1},{3,2},{4,3},{5,4},{6,5},{7,6},{8,15},{9,8},{10,9... | collective-permute-start | bytes 2359304 | tf_op jit(solution)/shard_map/ppermute | solution.py:39
  64.2 9.9 %collective-permute-start.11 = (bf16[9,128,128]{2,1,0:T(8,128)(2,1)S(1)}, bf16[9,128,128]{2,1,0:T(8,128)(2,1)S(1)}, u32[]{:S(2)}, u32[]{:S(2)}) collective-permute-start(bf16[9,128,128]{2,1,0:T(8,128)(2,1)S(1)} %collective-permute-done.8.rest_5_.rest_6_), channel_id=1, source_target_pairs={{0,24},{8,0},{16,8},{24,16},{1,25},{9,1},{17,9},{25,17},{2,26},{10... | collective-permute-start | bytes 884744 | tf_op jit(solution)/shard_map/ppermute | solution.py:39
